TPU v7x, 32 devices: a whole 2x2x4 slice. The times are simulated.
32 devices in a mesh: segment: 2 (over core), space: 16 (over z, y, x).
Axes of the slice: x: 2, y: 2, z: 4, core: 2. Of those that a mesh axis runs over, the one named last changes fastest.
Arguments:
- stash_down: bfloat16 [2, 64, 32, 384], P('segment', 'space'), may hold values from -6 to 6
- stash_up: bfloat16 [2, 64, 32, 384], P('segment', 'space'), may hold values from -6 to 6
- grad_down: bfloat16 [64, 32, 384], P('space'), may hold values from -6 to 6
- grad_up: bfloat16 [64, 32, 384], P('space'), may hold values from -6 to 6
- dw_kernel: bfloat16 [2, 2, 49, 384], P('segment'), as said below
- norm_gain: float32 [2, 2, 384], P('segment'), as said below
- norm_bias: float32 [2, 2, 384], P('segment'), as said below
- w_in: bfloat16 [2, 2, 384, 1536], P('segment', None, 'space'), as said below
- b_in: float32 [2, 2, 1536], P('segment'), as said below
- w_out: bfloat16 [2, 2, 1536, 384], P('segment', None, 'space'), as said below
- layer_scale: float32 [2, 2, 384], P('segment'), as said below
Outputs:
- input_grad_down: bfloat16 [2, 64, 32, 384], P('segment', 'space')
- input_grad_up: bfloat16 [2, 64, 32, 384], P('segment', 'space')
- w_out_grad: float32 [2, 1536, 384], P('segment', 'space')
- kernel_grad: float32 [2, 49, 384], P('segment')
Inputs may be any that keep to these rules, and one draw needn't show every extreme that they name: `dw_kernel`: entry [s, 1] equals entry [1 - s, 0] for every s. `norm_gain`: entry [s, 1] equals entry [1 - s, 0] for every s. `norm_bias`: entry [s, 1] equals entry [1 - s, 0] for every s. `w_in`: entry [s, 1] equals entry [1 - s, 0] for every s. `b_in`: entry [s, 1] equals entry [1 - s, 0] for every s. `w_out`: entry [s, 1] equals entry [1 - s, 0] for every s. `layer_scale`: entry [s, 1] equals entry [1 - s, 0] for every s.
All inputs are finite; a program needn't handle non-finite values.
Results may differ from a plain program's by a relative error of at most 0.0075.
Values may be sent and summed in bfloat16 or wider, within the bound.
A program may use at most 64 MiB of HBM per device.

v0:
```python
import math

import jax
import jax.numpy as jnp
from jax import lax
from jax.sharding import PartitionSpec as P

KSIDE = 7


def padded_2(cells, sides, width):
    for axis, dim in sides:
        count = lax.axis_size(axis)
        ends = count - 1
        head = lax.slice_in_dim(cells, 0, width, axis=dim)
        tail = lax.slice_in_dim(cells, cells.shape[dim] - width, cells.shape[dim], axis=dim)
        cells = jnp.concatenate(
            [
                lax.ppermute(tail, axis, [(i, (i + 1) % count) for i in range(ends)]),
                cells,
                lax.ppermute(head, axis, [((i + 1) % count, i) for i in range(ends)]),
            ],
            axis=dim,
        )
    return cells


def passed_along(shard, axis, by):
    devices = lax.axis_size(axis)
    pairs = [(i, i + by) for i in range(devices) if 0 <= i + by < devices]
    return lax.ppermute(shard, axis, pairs)


def as_sent(shard):
    return jax.tree.map(lambda a: a.astype(jnp.bfloat16) if a.dtype == jnp.float32 else a, shard)


def swapped(block, axis, stride):
    count = lax.axis_size(axis)
    route = []
    for low in range(count):
        high = low | 1 << stride
        if high != low and high < count:
            route += [(low, high), (high, low)]
    return lax.ppermute(block, axis, route)


def gelu_parts(a):
    inner = 0.7978845608 * (a + 0.044715 * a * a * a)
    th = jnp.tanh(inner)
    value = 0.5 * a * (1.0 + th)
    slope = 0.5 * (1.0 + th) + 0.5 * a * (1.0 - th * th) * 0.7978845608 * (1.0 + 0.134145 * a * a)
    return (value, slope)


def grouped_conv(padded, filters):
    chans = padded.shape[2]
    result = lax.conv_general_dilated(
        padded[None],
        filters,
        (1, 1),
        "VALID",
        dimension_numbers=("NHWC", "HWIO", "NHWC"),
        feature_group_count=chans,
        precision=lax.Precision.HIGHEST,
    )
    return result[0]


def depthwise(padded, kernel):
    chans = kernel.shape[1]
    filters = kernel.reshape(KSIDE, KSIDE, 1, chans)
    return grouped_conv(padded, filters)


def depthwise_back(padded, kernel):
    chans = kernel.shape[1]
    filters = kernel.reshape(KSIDE, KSIDE, 1, chans)[::-1, ::-1]
    return grouped_conv(padded, filters)


def kernel_terms(padded, grad):
    rows, cols, chans = grad.shape
    filters = grad.reshape(rows, cols, 1, chans)
    return grouped_conv(padded, filters).reshape(KSIDE * KSIDE, chans)


def pointwise_back(v, g, gain, bias, w_first, b_first, w_second, scale_res):
    rows, cols, chans = v.shape
    flat = v.reshape(rows * cols, chans)
    mean_v = jnp.mean(flat, axis=1, keepdims=True)
    centred = flat - mean_v
    rs = lax.rsqrt(jnp.mean(centred * centred, axis=1, keepdims=True) + 1e-06)
    nh = centred * rs
    normed = (nh * gain + bias).astype(jnp.bfloat16)
    pre = jnp.dot(normed, w_first, preferred_element_type=jnp.float32) + b_first
    value, slope = gelu_parts(pre)
    hidden = value.astype(jnp.bfloat16)
    outer = (g.reshape(rows * cols, chans).astype(jnp.float32) * scale_res).astype(jnp.bfloat16)
    dh = lax.dot_general(
        outer, w_second, (((1,), (1,)), ((), ())), preferred_element_type=jnp.float32
    )
    da = (dh * slope).astype(jnp.bfloat16)
    dn = lax.dot_general(da, w_first, (((1,), (1,)), ((), ())), preferred_element_type=jnp.float32)
    q = dn * gain
    du = rs * (
        q - jnp.mean(q, axis=1, keepdims=True) - nh * jnp.mean(q * nh, axis=1, keepdims=True)
    )
    return (du.astype(jnp.bfloat16).reshape(rows, cols, chans), hidden, outer)


def per_device(
    stash_down,
    stash_up,
    grad_down,
    grad_up,
    dw_kernel,
    norm_gain,
    norm_bias,
    w_in,
    b_in,
    w_out,
    layer_scale,
):
    segments = lax.axis_size("segment")
    me = lax.axis_index("segment")
    half = KSIDE // 2
    rows, cols, chans = (stash_down.shape[1], stash_down.shape[2], stash_down.shape[3])
    hidden_units = w_in.shape[3]
    norm = 1.0 / math.sqrt(2.0 * rows * lax.axis_size("space") * cols)
    w_in_all, w_out_all = (
        lax.all_gather(w_in, "space", axis=2, tiled=True),
        lax.all_gather(w_out, "space", axis=2, tiled=True),
    )
    x_down = stash_down[0]
    x_up = stash_up[0]
    rimmed_both = padded_2(jnp.stack([x_down, x_up]), (("space", 1),), half)
    down_in = grad_down
    up_in = grad_up
    out_down = jnp.zeros_like(grad_down)
    out_up = jnp.zeros_like(grad_up)
    tokens = rows * cols
    hid_down = jnp.zeros((tokens, hidden_units), jnp.bfloat16)
    hid_up = jnp.zeros((tokens, hidden_units), jnp.bfloat16)
    outer_down = jnp.zeros((tokens, chans), jnp.bfloat16)
    outer_up = jnp.zeros((tokens, chans), jnp.bfloat16)
    kern_down = jnp.zeros((KSIDE * KSIDE, chans), jnp.float32)
    kern_up = jnp.zeros((KSIDE * KSIDE, chans), jnp.float32)
    for step in range(segments):
        on_up = me == step
        on_down = me == segments - 1 - step
        active = jnp.logical_or(on_up, on_down)
        pick = on_up.astype(jnp.int32)

        def select(array):
            return lax.dynamic_index_in_dim(array[0], pick, 0, keepdims=False)

        rimmed = jnp.where(on_up, rimmed_both[1], rimmed_both[0])
        padded = jnp.pad(rimmed.astype(jnp.float32), ((0, 0), (half, half), (0, 0)))
        g = jnp.where(on_up, up_in, down_in)
        kern = select(dw_kernel).astype(jnp.float32)

        def front_live():
            v = depthwise(padded, kern)
            return pointwise_back(
                v,
                g,
                select(norm_gain),
                select(norm_bias),
                select(w_in_all),
                select(b_in),
                select(w_out_all),
                select(layer_scale),
            )

        def front_spare():
            return (
                jnp.zeros((rows, cols, chans), jnp.bfloat16),
                jnp.zeros((tokens, hidden_units), jnp.bfloat16),
                jnp.zeros((tokens, chans), jnp.bfloat16),
            )

        du, hidden, outer = lax.cond(active, front_live, front_spare)
        du_rimmed = padded_2(du, (("space", 0),), half)

        def back_live():
            du_pad = jnp.pad(du_rimmed.astype(jnp.float32), ((0, 0), (half, half), (0, 0)))
            dx_new = (g.astype(jnp.float32) + depthwise_back(du_pad, kern)).astype(jnp.bfloat16)
            dk_new = kernel_terms(padded, du.astype(jnp.float32))
            return (dx_new, dk_new)

        def back_spare():
            return (
                jnp.zeros((rows, cols, chans), jnp.bfloat16),
                jnp.zeros((KSIDE * KSIDE, chans), jnp.float32),
            )

        dx, dk = lax.cond(active, back_live, back_spare)
        out_down = jnp.where(on_down, dx, out_down)
        out_up = jnp.where(on_up, dx, out_up)
        kern_down = jnp.where(on_down, dk, kern_down)
        kern_up = jnp.where(on_up, dk, kern_up)
        hid_down = jnp.where(on_down, hidden, hid_down)
        hid_up = jnp.where(on_up, hidden, hid_up)
        outer_down = jnp.where(on_down, outer, outer_down)
        outer_up = jnp.where(on_up, outer, outer_up)
        if step + 1 < segments:
            down_in = passed_along(dx, "segment", -1)
            up_in = passed_along(dx, "segment", 1)
    levels = segments.bit_length() - 1
    for bit in range(levels):
        kern_up = swapped(as_sent(kern_up), "segment", bit).astype(kern_up.dtype)
    share = w_out.shape[2]
    joined = jnp.concatenate([hid_up, outer_up], axis=1)
    for bit in range(levels):
        joined = swapped(joined, "segment", bit)
    all_hidden = jnp.concatenate([hid_down, joined[:, :hidden_units]], axis=0)
    all_outer = jnp.concatenate([outer_down, joined[:, hidden_units:]], axis=0)
    columns = lax.slice_in_dim(all_hidden, 0, share * lax.axis_size("space"), axis=1)
    w_grad = lax.psum_scatter(
        lax.dot_general(
            columns, all_outer, (((0,), (0,)), ((), ())), preferred_element_type=jnp.float32
        )
        * norm,
        "space",
        scatter_dimension=0,
        tiled=True,
    )
    k_grad = lax.psum(kern_down + kern_up, "space") * norm
    return (out_down[None], out_up[None], w_grad[None], k_grad[None])


def solution(mesh):
    return jax.shard_map(
        per_device,
        mesh=mesh,
        in_specs=(
            P("segment", "space", None, None),
            P("segment", "space", None, None),
            P("space", None, None),
            P("space", None, None),
            P("segment", None, None, None),
            P("segment", None, None),
            P("segment", None, None),
            P("segment", None, "space", None),
            P("segment", None, None),
            P("segment", None, "space", None),
            P("segment", None, None),
        ),
        out_specs=(
            P("segment", "space", None, None),
            P("segment", "space", None, None),
            P("segment", "space", None),
            P("segment", None, None),
        ),
        check_vma=False,
    )
```

profile of v0, /device:TPU:0, one launch (start us, length us, event | category | flops | bytes accessed | tf_op | source)
XLA Modules:
  0.0 438.8 jit_solution(5692250722293077002)
XLA Ops:
  7.2 0.7 all-gather.3.cloned.1.call-update
  8.0 0.7 all-gather.5.cloned.1.call-update
  8.7 0.9 constant_dynamic-update-slice_fusion.1
  9.6 0.9 constant_dynamic-update-slice_fusion
  10.6 1.3 collective-permute-start.1
  11.9 5.5 %collective-permute-start = (bf16[2,3,32,384]{3,2,1,0:T(8,128)(2,1)S(1)}, bf16[2,3,32,384]{3,2,1,0:T(8,128)(2,1)S(1)}, u32[]{:S(2)}, u32[]{:S(2)}) collective-permute-start(bf16[2,3,32,384]{3,2,1,0:T(8,128)(2,1)S(1)} %get-tuple-element.140), channel_id=1, source_target_pairs={{0,1},{1,2},{2,3},{3,4},{4,5},{5,6},{6,7},{7,8},{8,9},{9,10},{10,1... | collective-permute-start | bytes 442376 | tf_op jit(solution)/shard_map/ppermute | solution.py:19
  17.4 1.1 constant_dynamic-slice_fusion
  18.5 0.9 broadcast_select_fusion.1
  19.5 5.1 %collective-permute-done = bf16[2,3,32,384]{3,2,1,0:T(8,128)(2,1)S(1)} collective-permute-done((bf16[2,3,32,384]{3,2,1,0:T(8,128)(2,1)S(1)}, bf16[2,3,32,384]{3,2,1,0:T(8,128)(2,1)S(1)}, u32[]{:S(2)}, u32[]{:S(2)}) %collective-permute-start) | collective-permute-done | bytes 147488 | tf_op jit(solution)/shard_map/ppermute | solution.py:19
  24.6 0.1 pad_maximum_fusion
  24.7 0.1 pad_convert_fusion.1
  24.8 51.0 %all-gather.3.cloned.1.call-done = bf16[1,2,1536,384]{3,2,1,0:T(8,128)(2,1)} async-done(((bf16[1,2,96,384]{3,2,1,0:T(8,128)(2,1)}), bf16[1,2,1536,384]{3,2,1,0:T(8,128)(2,1)}) %all-gather.3.cloned.1.call-update) | async-done | bytes 2359312 | tf_op jit(solution)/shard_map/all_gather | solution.py:133
  75.8 63.9 %all-gather.5.cloned.1.call-done = bf16[1,2,384,1536]{3,2,1,0:T(8,128)(2,1)} async-done(((bf16[1,2,24,1536]{3,2,1,0:T(8,128)(2,1)}), bf16[1,2,384,1536]{3,2,1,0:T(8,128)(2,1)}) %all-gather.5.cloned.1.call-update) | async-done | bytes 2359312 | tf_op jit(solution)/shard_map/all_gather | solution.py:132
  139.7 10.4 %conditional.4 = (bf16[4,32,384]{2,1,0:T(8,128)(2,1)S(1)}, bf16[128,1536]{1,0:T(8,128)(2,1)S(1)}, bf16[128,384]{1,0:T(8,128)(2,1)S(1)}) conditional(s32[]{:T(128)} %convert_element_type.123, () %tuple.42, (f32[10,38,384]{2,1,0:T(8,128)S(1)}, f32[49,384]{1,0:T(8,128)S(1)}, bf16[4,32,384]{2,1,0:T(8,128)(2,1)S(1)}, s32[]{:T(128)}, ...), branch_computations={%region_0.1_spmd, %region_1.6_spmd} | conditional | flops 488964224 | bytes 9116234 | solution.py:183
  139.7 0.1 reshape.228
  139.8 4.1 fusion.113
  143.9 0.9 multiply_reduce_fusion.1
  144.8 0.1 rsqrt.21
  144.9 0.1 div.21
  145.1 0.4 add_convert_fusion
  145.5 1.8 multiply_convert_fusion
  147.3 2.6 fusion.111
  149.9 0.1 multiply_convert_fusion.1
  150.1 1.3 collective-permute-start.3
  151.4 4.5 %collective-permute-start.2 = (bf16[3,32,384]{2,1,0:T(8,128)(2,1)S(1)}, bf16[3,32,384]{2,1,0:T(8,128)(2,1)S(1)}, u32[]{:S(2)}, u32[]{:S(2)}) collective-permute-start(bf16[3,32,384]{2,1,0:T(8,128)(2,1)S(1)} %get-tuple-element.144), channel_id=1, source_target_pairs={{0,1},{1,2},{2,3},{3,4},{4,5},{5,6},{6,7},{7,8},{8,9},{9,10},{10,1... | collective-permute-start | bytes 221192 | tf_op jit(solution)/shard_map/ppermute | solution.py:19
  156.0 0.4 collective-permute-done.3
  156.4 1.6 collective-permute-done.2
  158.0 4.3 conditional.5
  158.0 0.1 reshape.229
  158.1 0.1 pad_bitcast_fusion
  158.2 1.8 fusion.47
  160.0 2.3 convolution_reduce_fusion
  162.3 1.3 collective-permute-start.4
  163.6 1.3 collective-permute-start.5
  164.9 1.8 collective-permute-done.5
  166.8 10.4 %conditional.6 = (bf16[4,32,384]{2,1,0:T(8,128)(2,1)S(1)}, bf16[128,1536]{1,0:T(8,128)(2,1)S(1)}, bf16[128,384]{1,0:T(8,128)(2,1)S(1)}) conditional(s32[]{:T(128)} %convert_element_type.123, () %tuple.45, (f32[10,38,384]{2,1,0:T(8,128)S(1)}, f32[49,384]{1,0:T(8,128)S(1)}, bf16[4,32,384]{2,1,0:T(8,128)(2,1)S(1)}, s32[]{:T(128)}, ...), branch_computations={%region_8.9_spmd, %region_9.14_spmd} | conditional | flops 488964224 | bytes 9116234 | solution.py:183
  166.8 0.1 reshape.230
  166.9 4.1 fusion.116
  171.0 0.9 multiply_reduce_fusion.3
  171.9 0.1 rsqrt.23
  172.0 0.1 div.26
  172.2 0.4 add_convert_fusion.1
  172.6 1.8 multiply_convert_fusion.3
  174.4 2.6 fusion.112
  177.0 0.1 multiply_convert_fusion.4
  177.2 1.3 collective-permute-start.7
  178.5 4.9 %collective-permute-start.6 = (bf16[3,32,384]{2,1,0:T(8,128)(2,1)S(1)}, bf16[3,32,384]{2,1,0:T(8,128)(2,1)S(1)}, u32[]{:S(2)}, u32[]{:S(2)}) collective-permute-start(bf16[3,32,384]{2,1,0:T(8,128)(2,1)S(1)} %get-tuple-element.142), channel_id=1, source_target_pairs={{0,1},{1,2},{2,3},{3,4},{4,5},{5,6},{6,7},{7,8},{8,9},{9,10},{10,1... | collective-permute-start | bytes 221192 | tf_op jit(solution)/shard_map/ppermute | solution.py:19
  183.6 0.1 collective-permute-start.8
  183.7 0.4 collective-permute-done.7
  184.1 2.8 collective-permute-done.6
  186.9 4.3 conditional.7
  186.9 0.1 reshape.231
  187.0 0.1 pad_bitcast_fusion.1
  187.1 1.8 fusion.98
  188.9 2.2 convolution_reduce_fusion.1
  191.2 0.1 collective-permute-start.9
  191.2 1.2 collective-permute-done.9
  192.5 0.6 convert_add_fusion
  193.2 2.0 convolution_multiply_fusion.2
  195.3 0.7 select_bitcast_fusion.2
  196.0 103.2 %all-reduce.6.cloned.1.call-done = f32[49,384]{1,0:T(8,128)} async-done(((f32[49,384]{1,0:T(8,128)}), f32[49,384]{1,0:T(8,128)}) %all-reduce.6.cloned.1.call-update) | async-done | bytes 75280 | tf_op jit(solution)/shard_map/psum | solution.py:229
  299.2 0.9 broadcast_multiply_fusion.6
  300.1 0.7 broadcast_in_dim.57
  300.8 131.5 %reduce-scatter.2.cloned.1.call-done = f32[96,384]{1,0:T(8,128)} async-done(((f32[1536,384]{1,0:T(8,128)}), f32[96,384]{1,0:T(8,128)}) %reduce-scatter.2.cloned.1.call-update) | async-done | bytes 147472 | tf_op jit(solution)/shard_map/reduce_scatter | solution.py:220
  (59 shorter events, 1.1 us)
Async XLA Ops:
  7.2 68.6 %all-gather.3.cloned.1.call-start = ((), (), s32[]{:S(2)}) async-start(), calls=%async_computation.1 | async-start | bytes 2506752 | tf_op jit(solution)/shard_map/all_gather | solution.py:133
  7.9 131.8 %copy-start = (f32[1,2,1536]{2,1,0:T(2,128)S(1)}, f32[1,2,1536]{2,1,0:T(2,128)}, u32[]{:S(2)}) copy-start(f32[1,2,1536]{2,1,0:T(2,128)} %param.27) | copy-start | bytes 36868
  7.9 131.8 %copy-start.1 = (f32[1,2,384]{2,1,0:T(2,128)S(1)}, f32[1,2,384]{2,1,0:T(2,128)}, u32[]{:S(2)}) copy-start(f32[1,2,384]{2,1,0:T(2,128)} %param.29) | copy-start | bytes 9220
  7.9 131.7 %copy-start.2 = (f32[1,2,384]{2,1,0:T(2,128)S(1)}, f32[1,2,384]{2,1,0:T(2,128)}, u32[]{:S(2)}) copy-start(f32[1,2,384]{2,1,0:T(2,128)} %param.24) | copy-start | bytes 9220
  7.9 131.7 %copy-start.3 = (f32[1,2,384]{2,1,0:T(2,128)S(1)}, f32[1,2,384]{2,1,0:T(2,128)}, u32[]{:S(2)}) copy-start(f32[1,2,384]{2,1,0:T(2,128)} %param.25) | copy-start | bytes 9220
  7.9 131.7 %all-gather.5.cloned.1.call-start = ((), (), s32[]{:S(2)}) async-start(), calls=%async_computation.2 | async-start | bytes 2506752 | tf_op jit(solution)/shard_map/all_gather | solution.py:132
  8.7 290.5 %all-reduce.6.cloned.1.call-start = ((), (), s32[]{:S(2)}) async-start(), calls=%async_computation.4 | async-start | bytes 172032 | tf_op jit(solution)/shard_map/psum | solution.py:229
  10.6 8.9 %collective-permute-start.1 = (bf16[2,3,32,384]{3,2,1,0:T(8,128)(2,1)S(1)}, bf16[2,3,32,384]{3,2,1,0:T(8,128)(2,1)S(1)}, u32[]{:S(2)}, u32[]{:S(2)}) collective-permute-start(bf16[2,3,32,384]{3,2,1,0:T(8,128)(2,1)S(1)} %get-tuple-element.141), channel_id=1, source_target_pairs={{1,0},{2,1},{3,2},{4,3},{5,4},{6,5},{7,6},{8,7},{9,8},{10,9},{11,1... | collective-permute-start | bytes 442376 | tf_op jit(solution)/shard_map/ppermute | solution.py:21
  11.9 12.7 %collective-permute-start = (bf16[2,3,32,384]{3,2,1,0:T(8,128)(2,1)S(1)}, bf16[2,3,32,384]{3,2,1,0:T(8,128)(2,1)S(1)}, u32[]{:S(2)}, u32[]{:S(2)}) collective-permute-start(bf16[2,3,32,384]{3,2,1,0:T(8,128)(2,1)S(1)} %get-tuple-element.140), channel_id=1, source_target_pairs={{0,1},{1,2},{2,3},{3,4},{4,5},{5,6},{6,7},{7,8},{8,9},{9,10},{10,1... | collective-permute-start | bytes 442376 | tf_op jit(solution)/shard_map/ppermute | solution.py:19
  150.1 6.2 %collective-permute-start.3 = (bf16[3,32,384]{2,1,0:T(8,128)(2,1)S(1)}, bf16[3,32,384]{2,1,0:T(8,128)(2,1)S(1)}, u32[]{:S(2)}, u32[]{:S(2)}) collective-permute-start(bf16[3,32,384]{2,1,0:T(8,128)(2,1)S(1)} %get-tuple-element.145), channel_id=1, source_target_pairs={{1,0},{2,1},{3,2},{4,3},{5,4},{6,5},{7,6},{8,7},{9,8},{10,9},{11,1... | collective-permute-start | bytes 221192 | tf_op jit(solution)/shard_map/ppermute | solution.py:21
  151.4 6.5 %collective-permute-start.2 = (bf16[3,32,384]{2,1,0:T(8,128)(2,1)S(1)}, bf16[3,32,384]{2,1,0:T(8,128)(2,1)S(1)}, u32[]{:S(2)}, u32[]{:S(2)}) collective-permute-start(bf16[3,32,384]{2,1,0:T(8,128)(2,1)S(1)} %get-tuple-element.144), channel_id=1, source_target_pairs={{0,1},{1,2},{2,3},{3,4},{4,5},{5,6},{6,7},{7,8},{8,9},{9,10},{10,1... | collective-permute-start | bytes 221192 | tf_op jit(solution)/shard_map/ppermute | solution.py:19
  162.3 2.7 collective-permute-start.4
  163.6 3.2 collective-permute-start.5
  177.2 6.9 %collective-permute-start.7 = (bf16[3,32,384]{2,1,0:T(8,128)(2,1)S(1)}, bf16[3,32,384]{2,1,0:T(8,128)(2,1)S(1)}, u32[]{:S(2)}, u32[]{:S(2)}) collective-permute-start(bf16[3,32,384]{2,1,0:T(8,128)(2,1)S(1)} %get-tuple-element.143), channel_id=1, source_target_pairs={{1,0},{2,1},{3,2},{4,3},{5,4},{6,5},{7,6},{8,7},{9,8},{10,9},{11,1... | collective-permute-start | bytes 221192 | tf_op jit(solution)/shard_map/ppermute | solution.py:21
  178.5 8.3 %collective-permute-start.6 = (bf16[3,32,384]{2,1,0:T(8,128)(2,1)S(1)}, bf16[3,32,384]{2,1,0:T(8,128)(2,1)S(1)}, u32[]{:S(2)}, u32[]{:S(2)}) collective-permute-start(bf16[3,32,384]{2,1,0:T(8,128)(2,1)S(1)} %get-tuple-element.142), channel_id=1, source_target_pairs={{0,1},{1,2},{2,3},{3,4},{4,5},{5,6},{6,7},{7,8},{8,9},{9,10},{10,1... | collective-permute-start | bytes 221192 | tf_op jit(solution)/shard_map/ppermute | solution.py:19
  183.6 9.6 %collective-permute-start.8 = (bf16[128,1920]{1,0:T(8,128)(2,1)S(1)}, bf16[128,1920]{1,0:T(8,128)(2,1)S(1)}, u32[]{:S(2)}, u32[]{:S(2)}) collective-permute-start(bf16[128,1920]{1,0:T(8,128)(2,1)S(1)} %pad_maximum_fusion.1), channel_id=1, source_target_pairs={{0,16},{16,0},{1,17},{17,1},{2,18},{18,2},{3,19},{19,3},{4,20},{20... | collective-permute-start | bytes 1474568 | tf_op jit(solution)/shard_map/ppermute | solution.py:45
  191.2 1.3 collective-permute-start.9
  193.1 239.2 %reduce-scatter.2.cloned.1.call-start = ((), (), s32[]{:S(2)}) async-start(), calls=%async_computation.3 | async-start | bytes 2506752 | tf_op jit(solution)/shard_map/reduce_scatter | solution.py:220
Sparse Core Ops, SparseCore 0:
  10.7 65.0 all-gather.2
  78.5 61.1 all-gather.4
  193.2 105.9 all-reduce.5
  304.5 127.6 reduce-scatter.1
where the time goes:
time: 439 us
  waiting for transfers between devices  364 us (83%)
  matrix products  27 us (6%)
  starting transfers between devices  21.7 us (5%)
  between operations  14.1 us (3%)
  other arithmetic  6.63 us (2%)
  local copies, waits for them, and re-layouts  4.77 us (1%)
    reduce_scatter x1, waiting for transfers between devices, per_device(): lax.psum_scatter(lax.dot_general(columns, all_outer, (((0,), (0,)), ((),...  131 us
    psum x1, waiting for transfers between devices, per_device(): k_grad = lax.psum(kern_down + kern_up, 'space') * norm  103 us
    all_gather x1, waiting for transfers between devices, per_device(): lax.all_gather(w_in, 'space', axis=2, tiled=True)  63.9 us
    all_gather x1, waiting for transfers between devices, per_device(): lax.all_gather(w_out, 'space', axis=2, tiled=True)  51 us
    conv_general_dilated x6, matrix products, grouped_conv(): lax.conv_general_dilated(padded[None], filters, (1, 1), 'VALID', dimensio...  16.2 us
    ppermute x3, starting transfers between devices, padded_2(): lax.ppermute(tail, axis, [(i, (i + 1) % count) for i in range(ends)])  14.9 us
    ppermute x3, waiting for transfers between devices, padded_2(): lax.ppermute(tail, axis, [(i, (i + 1) % count) for i in range(ends)])  9.47 us
  transfers between devices with their start and end apart: 14, of which 11 were waited for; matrix products, arithmetic and copies ran while one was open for 3% of the time, Pallas kernels for 0%

commit v1 on v0

--- a/solution.py
+++ b/solution.py
@@ -1,11 +1,289 @@
+import functools
 import math
 
 import jax
 import jax.numpy as jnp
 from jax import lax
+from jax.experimental import pallas as pl
+from jax.experimental.pallas import tpu as pltpu
 from jax.sharding import PartitionSpec as P
 
 KSIDE = 7
+
+
+MESH = pl.DeviceIdType.MESH
+
+
+def turned(q):
+    return q + (q // 2) * (1 - 2 * (q % 2))
+
+
+def chip_at(k):
+    q = k // 4
+    r = k % 4
+    odd = q % 2
+    z = r + odd * (3 - 2 * r)
+    return z * 4 + turned(q)
+
+
+def place_of(p):
+    z = p // 4
+    q = turned(p % 4)
+    odd = q % 2
+    return q * 4 + z + odd * (3 - 2 * z)
+
+
+def gather_kernel(
+    n, win, wout, win_all, wout_all, own_sem, send_sem, recv_sem, over_send, over_recv
+):
+    core = lax.axis_index("segment")
+    p = lax.axis_index("space")
+    k = place_of(p)
+    ways = (chip_at((k + 1) % n), chip_at((k + n - 1) % n))
+    barrier = pltpu.get_barrier_semaphore()
+    for device in ((core, ways[0]), (core, ways[1]), (1 - core, p)):
+        pl.semaphore_signal(barrier, inc=1, device_id=device, device_id_type=MESH)
+    pl.semaphore_wait(barrier, 3)
+
+    half = n // 2
+    steps = [
+        (t, b, d) for t in range(half) for b in (1, 0) for d in (0, 1) if t < half - 1 or b != d
+    ]
+
+    def carry(mine, mine_all, other_all, mine_slot):
+        def hop(t, b, d):
+            origin = chip_at((k + (n - t if d == 0 else t)) % n)
+            spot = mine_all.at[b, origin]
+            return pltpu.make_async_remote_copy(
+                src_ref=mine.at[mine_slot(b)] if t == 0 else spot,
+                dst_ref=spot,
+                send_sem=send_sem.at[t, b, d],
+                recv_sem=recv_sem.at[t, b, d],
+                device_id=(core, ways[d]),
+                device_id_type=MESH,
+            )
+
+        def arrival(t, b, d):
+            origin = chip_at((k + (n - t - 1 if d == 0 else t + 1)) % n)
+            return mine_all.at[b, origin], other_all.at[b, origin]
+
+        def across(t, b, d):
+            spot, _ = arrival(t, b, d)
+            return pltpu.make_async_remote_copy(
+                src_ref=spot,
+                dst_ref=spot,
+                send_sem=over_send.at[t, b, d],
+                recv_sem=over_recv.at[t, b, d],
+                device_id=(1 - core, p),
+                device_id_type=MESH,
+            )
+
+        for b in (1, 0):
+            for d in (0, 1):
+                hop(0, b, d).start()
+        for t, b, d in steps:
+            spot, _ = arrival(t, b, d)
+            pltpu.make_async_copy(spot, spot, recv_sem.at[t, b, d]).wait()
+            if (t + 1, b, d) in steps:
+                hop(t + 1, b, d).start()
+            across(t, b, d).start()
+        for t, b, d in steps:
+            hop(t, b, d).wait_send()
+            across(t, b, d).wait_send()
+            _, other = arrival(t, b, d)
+            pltpu.make_async_copy(other, other, over_recv.at[t, b, d]).wait()
+
+    def own(slot):
+        copies = []
+        for b in (0, 1):
+            copies.append(pltpu.make_async_copy(win.at[slot(b)], win_all.at[b, p], own_sem.at[0, b]))
+            copies.append(
+                pltpu.make_async_copy(wout.at[slot(b)], wout_all.at[b, p], own_sem.at[1, b])
+            )
+        return copies
+
+    @pl.when(core == 0)
+    def _():
+        for c in own(lambda b: b):
+            c.start()
+        carry(win, win_all, wout_all, lambda b: b)
+        for c in own(lambda b: b):
+            c.wait()
+
+    @pl.when(core == 1)
+    def _():
+        for c in own(lambda b: 1 - b):
+            c.start()
+        carry(wout, wout_all, win_all, lambda b: 1 - b)
+        for c in own(lambda b: 1 - b):
+            c.wait()
+
+
+def gathered(w_in, w_out):
+    n = lax.axis_size("space")
+    win, wout = w_in[0], w_out[0]
+    sems = pltpu.SemaphoreType.DMA((n // 2, 2, 2))
+    win_all, wout_all = pl.pallas_call(
+        functools.partial(gather_kernel, n),
+        out_shape=(
+            jax.ShapeDtypeStruct((2, n) + win.shape[1:], win.dtype),
+            jax.ShapeDtypeStruct((2, n) + wout.shape[1:], wout.dtype),
+        ),
+        in_specs=[pl.BlockSpec(memory_space=pl.ANY)] * 2,
+        out_specs=(pl.BlockSpec(memory_space=pl.ANY),) * 2,
+        scratch_shapes=[pltpu.SemaphoreType.DMA((2, 2)), sems, sems, sems, sems],
+        compiler_params=pltpu.CompilerParams(collective_id=0, has_side_effects=True),
+        name="gather_weights",
+    )(win, wout)
+    return (
+        win_all.reshape(2, n * win.shape[1], win.shape[2]),
+        wout_all.reshape(2, n * wout.shape[1], wout.shape[2]),
+    )
+
+
+def sum_kernel(
+    part,
+    dk,
+    out,
+    dk_out,
+    sa1,
+    sb1,
+    ra1,
+    rb1,
+    sa2,
+    sb2,
+    ra2,
+    rb2,
+    s3,
+    r3,
+    kr1,
+    ks2,
+    kr2,
+    ks3,
+    kr3,
+    send_sem,
+    recv_sem,
+):
+    core = lax.axis_index("segment")
+    p = lax.axis_index("space")
+    z = p // 4
+    y = (p // 2) % 2
+    x = p % 2
+    half = out.shape[0] // 2
+    over_x = (core, z * 4 + y * 2 + 1 - x)
+    over_y = (core, z * 4 + (1 - y) * 2 + x)
+    over_z = [(core, ((z + j) % 4) * 4 + y * 2 + x) for j in (1, 2, 3)]
+    barrier = pltpu.get_barrier_semaphore()
+    for device in [over_x, over_y] + over_z:
+        pl.semaphore_signal(barrier, inc=1, device_id=device, device_id_type=MESH)
+
+    def sent(src, dst, number, device):
+        return pltpu.make_async_remote_copy(
+            src_ref=src,
+            dst_ref=dst,
+            send_sem=send_sem.at[number],
+            recv_sem=recv_sem.at[number],
+            device_id=device,
+            device_id_type=MESH,
+        )
+
+    low, high = pl.ds(0, half), pl.ds(half, half)
+    for zz in range(4):
+        for o in range(2):
+            sa1[zz, o] = part[zz, o, 1 - x, low].astype(sa1.dtype)
+            sb1[zz, o] = part[zz, 1 - y, o, high].astype(sb1.dtype)
+    pl.semaphore_wait(barrier, 5)
+    first = [sent(sa1, ra1, 0, over_x), sent(sb1, rb1, 1, over_y), sent(dk, kr1, 2, over_x)]
+    for c in first:
+        c.start()
+    for c in first:
+        c.wait_recv()
+    for zz in range(4):
+        sa2[zz] = (part[zz, 1 - y, x, low] + ra1[zz, 1 - y].astype(jnp.float32)).astype(sa2.dtype)
+        sb2[zz] = (part[zz, y, 1 - x, high] + rb1[zz, 1 - x].astype(jnp.float32)).astype(sb2.dtype)
+    ks2[...] = dk[...] + kr1[...]
+    second = [sent(sa2, ra2, 3, over_y), sent(sb2, rb2, 4, over_x), sent(ks2, kr2, 5, over_y)]
+    for c in second:
+        c.start()
+
+    def kept(zz):
+        a = part[zz, y, x, low] + ra1[zz, y].astype(jnp.float32)
+        b = part[zz, y, x, high] + rb1[zz, x].astype(jnp.float32)
+        return a, b
+
+    for c in second:
+        c.wait_recv()
+    ksum = ks2[...] + kr2[...]
+    ks3[...] = ksum.astype(ks3.dtype)
+    third = []
+    for j in (1, 2, 3):
+        zz = (z + j) % 4
+        a, b = kept(zz)
+        s3[j - 1, low] = (a + ra2[zz].astype(jnp.float32)).astype(s3.dtype)
+        s3[j - 1, high] = (b + rb2[zz].astype(jnp.float32)).astype(s3.dtype)
+        third.append(sent(s3.at[j - 1], r3.at[j - 1], 6 + j, over_z[j - 1]))
+        third.append(sent(ks3, kr3.at[j - 1], 9 + j, over_z[j - 1]))
+        third[-2].start()
+        third[-1].start()
+    a, b = kept(z)
+    a = a + ra2[z].astype(jnp.float32)
+    b = b + rb2[z].astype(jnp.float32)
+    for c in third:
+        c.wait_recv()
+    for j in range(3):
+        a = a + r3[j, low].astype(jnp.float32)
+        b = b + r3[j, high].astype(jnp.float32)
+        ksum = ksum + kr3[j].astype(jnp.float32)
+    out[low] = a
+    out[high] = b
+    dk_out[...] = ksum
+    for c in first + second + third:
+        c.wait_send()
+
+
+def summed(part, dk):
+    n = lax.axis_size("space")
+    share, chans = part.shape[0] // n, part.shape[1]
+    part = part.reshape(4, 2, 2, share, chans)
+    taps = dk.shape[0]
+    dk = jnp.pad(dk, ((0, -taps % 16), (0, 0)))
+    half = share // 2
+    sent = jnp.bfloat16
+    wide = pltpu.VMEM((4, 2, half, chans), sent)
+    narrow = pltpu.VMEM((4, half, chans), sent)
+    out, dk = pl.pallas_call(
+        sum_kernel,
+        out_shape=(
+            jax.ShapeDtypeStruct((share, chans), jnp.float32),
+            jax.ShapeDtypeStruct(dk.shape, jnp.float32),
+        ),
+        in_specs=[pl.BlockSpec(memory_space=pltpu.VMEM)] * 2,
+        out_specs=(pl.BlockSpec(memory_space=pltpu.VMEM),) * 2,
+        scratch_shapes=[
+            wide,
+            wide,
+            wide,
+            wide,
+            narrow,
+            narrow,
+            narrow,
+            narrow,
+            pltpu.VMEM((3, share, chans), sent),
+            pltpu.VMEM((3, share, chans), sent),
+            pltpu.VMEM(dk.shape, jnp.float32),
+            pltpu.VMEM(dk.shape, jnp.float32),
+            pltpu.VMEM(dk.shape, jnp.float32),
+            pltpu.VMEM(dk.shape, sent),
+            pltpu.VMEM((3,) + dk.shape, sent),
+            pltpu.SemaphoreType.DMA((13,)),
+            pltpu.SemaphoreType.DMA((13,)),
+        ],
+        compiler_params=pltpu.CompilerParams(
+            collective_id=1, has_side_effects=True, vmem_limit_bytes=24 * 1024 * 1024
+        ),
+        name="sum_gradients",
+    )(part, dk)
+    return out, dk[:taps]
 
 
 def padded_2(cells, sides, width):
@@ -128,10 +406,14 @@
     rows, cols, chans = (stash_down.shape[1], stash_down.shape[2], stash_down.shape[3])
     hidden_units = w_in.shape[3]
     norm = 1.0 / math.sqrt(2.0 * rows * lax.axis_size("space") * cols)
-    w_in_all, w_out_all = (
-        lax.all_gather(w_in, "space", axis=2, tiled=True),
-        lax.all_gather(w_out, "space", axis=2, tiled=True),
-    )
+    paired = segments == 2 and lax.axis_size("space") == 16
+    if paired:
+        w_in_all, w_out_all = gathered(w_in, w_out)
+    else:
+        w_in_all, w_out_all = (
+            lax.all_gather(w_in, "space", axis=2, tiled=True)[0],
+            lax.all_gather(w_out, "space", axis=2, tiled=True)[0],
+        )
     x_down = stash_down[0]
     x_up = stash_up[0]
     rimmed_both = padded_2(jnp.stack([x_down, x_up]), (("space", 1),), half)
@@ -160,6 +442,11 @@
         g = jnp.where(on_up, up_in, down_in)
         kern = select(dw_kernel).astype(jnp.float32)
 
+        def chosen(array):
+            if paired:
+                return array[segments - 1 - step]
+            return lax.dynamic_index_in_dim(array, pick, 0, keepdims=False)
+
         def front_live():
             v = depthwise(padded, kern)
             return pointwise_back(
@@ -167,9 +454,9 @@
                 g,
                 select(norm_gain),
                 select(norm_bias),
-                select(w_in_all),
+                chosen(w_in_all),
                 select(b_in),
-                select(w_out_all),
+                chosen(w_out_all),
                 select(layer_scale),
             )
 
@@ -180,7 +467,7 @@
                 jnp.zeros((tokens, chans), jnp.bfloat16),
             )
 
-        du, hidden, outer = lax.cond(active, front_live, front_spare)
+        du, hidden, outer = front_live() if paired else lax.cond(active, front_live, front_spare)
         du_rimmed = padded_2(du, (("space", 0),), half)
 
         def back_live():
@@ -195,7 +482,7 @@
                 jnp.zeros((KSIDE * KSIDE, chans), jnp.float32),
             )
 
-        dx, dk = lax.cond(active, back_live, back_spare)
+        dx, dk = back_live() if paired else lax.cond(active, back_live, back_spare)
         out_down = jnp.where(on_down, dx, out_down)
         out_up = jnp.where(on_up, dx, out_up)
         kern_down = jnp.where(on_down, dk, kern_down)
@@ -217,16 +504,18 @@
     all_hidden = jnp.concatenate([hid_down, joined[:, :hidden_units]], axis=0)
     all_outer = jnp.concatenate([outer_down, joined[:, hidden_units:]], axis=0)
     columns = lax.slice_in_dim(all_hidden, 0, share * lax.axis_size("space"), axis=1)
-    w_grad = lax.psum_scatter(
+    w_part = (
         lax.dot_general(
             columns, all_outer, (((0,), (0,)), ((), ())), preferred_element_type=jnp.float32
         )
-        * norm,
-        "space",
-        scatter_dimension=0,
-        tiled=True,
+        * norm
     )
-    k_grad = lax.psum(kern_down + kern_up, "space") * norm
+    k_part = (kern_down + kern_up) * norm
+    if paired:
+        w_grad, k_grad = summed(w_part, k_part)
+    else:
+        w_grad = lax.psum_scatter(w_part, "space", scatter_dimension=0, tiled=True)
+        k_grad = lax.psum(k_part, "space")
     return (out_down[None], out_up[None], w_grad[None], k_grad[None])
 
 

time: 439 us -> 149 us (0.34)
  waiting for transfers between devices: 364 us -> 0.75 us
  Pallas kernels: 0 us -> 76.3 us
  between operations: 14.1 us -> 1.26 us
  local copies, waits for them, and re-layouts: 4.77 us -> 14 us
    reduce_scatter x1 -> x0, waiting for transfers between devices: 131 us -> none  [per_device(): lax.psum_scatter(lax.dot_general(columns, all_outer, (((0,), (0,)), ((),...]
    all_gather x2 -> x0, waiting for transfers between devices: 115 us -> none  [the longest x1 63.9 us: per_device(): lax.all_gather(w_in, 'space', axis=2, tiled=True)]
    psum x1 -> x0, waiting for transfers between devices: 103 us -> none  [per_device(): k_grad = lax.psum(kern_down + kern_up, 'space') * norm]
    pallas_call x0 -> x2, Pallas kernels: none -> 76.3 us  [the longest x1 43.9 us: gathered(): pl.pallas_call(functools.partial(gather_kernel, n), out_shape=(jax.ShapeD...]
    ppermute x3, waiting for transfers between devices: 9.47 us -> 0.01 us  [padded_2(): lax.ppermute(tail, axis, [(i, (i + 1) % count) for i in range(ends)])]
  transfers between devices with their start and end apart: 14 -> 10, of which waited for: 11 -> 1; matrix products, arithmetic and copies ran while one was open for 3% -> 15% of each run, Pallas kernels for 0% -> 30%
where the time goes in v1:
time: 149 us
  Pallas kernels  76.3 us (51%)
  matrix products  24.8 us (17%)
  starting transfers between devices  23.6 us (16%)
  local copies, waits for them, and re-layouts  14 us (9%)
  other arithmetic  7.77 us (5%)
    pallas_call x1, Pallas kernels, gathered(): pl.pallas_call(functools.partial(gather_kernel, n), out_shape=(jax.ShapeD...  43.9 us
    pallas_call x1, Pallas kernels, summed(): pl.pallas_call(sum_kernel, out_shape=(jax.ShapeDtypeStruct((share, chans)...  32.4 us
    conv_general_dilated x6, matrix products, grouped_conv(): lax.conv_general_dilated(padded[None], filters, (1, 1), 'VALID', dimensio...  16.3 us
    ppermute x3, starting transfers between devices, padded_2(): lax.ppermute(tail, axis, [(i, (i + 1) % count) for i in range(ends)])  14.8 us
    dot_general x2, matrix products, pointwise_back(): lax.dot_general(da, w_first, (((1,), (1,)), ((), ())), preferred_element_...  5.63 us
    ppermute x3, starting transfers between devices, padded_2(): lax.ppermute(head, axis, [((i + 1) % count, i) for i in range(ends)])  3.88 us
    ppermute x2, starting transfers between devices, passed_along(): return lax.ppermute(shard, axis, pairs)  3.6 us
    slice x2, local copies, waits for them, and re-layouts, chosen(): return array[segments - 1 - step]  3.58 us
  transfers between devices with their start and end apart: 10, of which 1 were waited for; matrix products, arithmetic and copies ran while one was open for 15% of the time, Pallas kernels for 30%

profile of v1, /device:TPU:0, one launch (start us, length us, event | category | flops | bytes accessed | tf_op | source)
XLA Modules:
  0.0 148.5 jit_solution(4540008373279163092)
XLA Ops:
  0.6 0.9 constant_dynamic-update-slice_fusion.1
  1.5 0.9 constant_dynamic-update-slice_fusion
  2.5 1.3 collective-permute-start.1
  3.8 5.5 %collective-permute-start = (bf16[2,3,32,384]{3,2,1,0:T(8,128)(2,1)S(1)}, bf16[2,3,32,384]{3,2,1,0:T(8,128)(2,1)S(1)}, u32[]{:S(2)}, u32[]{:S(2)}) collective-permute-start(bf16[2,3,32,384]{3,2,1,0:T(8,128)(2,1)S(1)} %get-tuple-element.50), channel_id=1, source_target_pairs={{0,1},{1,2},{2,3},{3,4},{4,5},{5,6},{6,7},{7,8},{8,9},{9,10},{10,1... | collective-permute-start | bytes 442376 | tf_op jit(solution)/shard_map/ppermute | solution.py:297
  9.3 43.9 %gather_weights.1 = (bf16[2,16,24,1536]{3,2,1,0:T(8,128)(2,1)}, bf16[2,16,96,384]{3,2,1,0:T(8,128)(2,1)}) custom-call(bf16[2,24,1536]{2,1,0:T(8,128)(2,1)} %bitcast.111, bf16[2,96,384]{2,1,0:T(8,128)(2,1)} %bitcast.112), custom_call_target="tpu_custom_call" | custom-call | tf_op jit(solution)/shard_map/gather_weights/pallas_call | solution.py:126
  53.2 1.9 %fusion.97 = (bf16[1,16,24,1536]{3,2,1,0:T(8,128)(2,1)S(1)}, bf16[1,16,24,1536]{3,2,1,0:T(8,128)(2,1)S(1)}) fusion(bf16[2,16,24,1536]{3,2,1,0:T(8,128)(2,1)} %get-tuple-element.9), kind=kLoop, calls=%fused_computation.166 | loop fusion | bytes 4718592 | tf_op jit(solution)/shard_map/slice | solution.py:447
  55.2 0.4 copy-done
  55.6 0.0 copy-start.21
  55.6 0.0 copy-start.14
  55.6 0.0 copy-start.7
  55.6 1.6 %fusion.96 = (bf16[1,16,96,384]{3,2,1,0:T(8,128)(2,1)}, bf16[1,16,96,384]{3,2,1,0:T(8,128)(2,1)}) fusion(bf16[2,16,96,384]{3,2,1,0:T(8,128)(2,1)S(1)} %copy-done), kind=kLoop, calls=%fused_computation.165 | loop fusion | bytes 4718592 | tf_op jit(solution)/shard_map/slice | solution.py:447
  57.3 0.6 fusion.80
  57.9 0.7 multiply_convert_fusion.5
  58.5 0.6 fusion.82
  59.2 0.6 dynamic-slice_reduce_fusion
  59.8 0.8 constant_dynamic-slice_fusion.3
  60.6 0.0 collective-permute-done.1
  60.6 0.0 collective-permute-done
  60.6 0.1 pad_maximum_fusion
  60.7 0.1 select_bitcast_fusion
  60.7 0.9 pad_bitcast_fusion
  61.7 4.1 %fusion.101 = (f32[4,32]{1,0:T(4,128)S(1)}, f32[1,4,32,384]{3,0,2,1:T(1,128)S(1)}) fusion(bf16[7,7,1,384]{3,2,1,0:T(2,128)(2,1)S(1)} %bitcast.118, bf16[1,10,38,384]{3,2,1,0:T(8,128)(2,1)S(1)} %get-tuple-element.70), kind=kOutput, calls=%fused_computation.170 | convolution fusion | flops 4865920 | bytes 526592 | tf_op jit(solution)/shard_map/conv_general_dilated | solution.py:336
  65.8 0.6 div.31
  66.4 0.9 multiply_reduce_fusion.3
  67.3 0.6 rsqrt.25
  67.9 0.4 add_convert_fusion.1
  68.3 0.4 convolution_add_fusion.1
  68.7 2.9 %fusion.95 = (f32[128]{0:T(128)S(1)}, f32[128]{0:T(128)S(1)}, f32[128,384]{1,0:T(8,128)}) fusion(f32[128]{0:T(128)} %rsqrt.25, f32[128]{0:T(128)} %div.31, f32[1,4,32,384]{3,2,0,1:T(8,128)S(1)} %copy.37, f32[384]{0:T(512)} %copy-done.17, bf16[384,1536]{1,0:T(8,128)(2,1)S(1)} %bitcast.101, bf16[128,384]{1,0:T(8,128)(2,1)} %bitcast.114, ...), kind=kOutput, calls=%fused_computation.164 | convolution fusion | flops 306020096 | bytes 3640832 | tf_op jit(solution)/shard_map/dot_general | solution.py:382
  71.6 1.1 multiply_convert_fusion.4
  72.7 1.3 collective-permute-start.3
  74.0 4.5 %collective-permute-start.2 = (bf16[3,32,384]{2,1,0:T(8,128)(2,1)S(1)}, bf16[3,32,384]{2,1,0:T(8,128)(2,1)S(1)}, u32[]{:S(2)}, u32[]{:S(2)}) collective-permute-start(bf16[3,32,384]{2,1,0:T(8,128)(2,1)S(1)} %bitcast.122), channel_id=1, source_target_pairs={{0,1},{1,2},{2,3},{3,4},{4,5},{5,6},{6,7},{7,8},{8,9},{9,10},{10,1... | collective-permute-start | bytes 221192 | tf_op jit(solution)/shard_map/ppermute | solution.py:297
  78.6 3.6 %fusion.102 = (f32[4,32]{1,0:T(4,128)S(1)}, f32[1,4,32,384]{3,0,2,1:T(1,128)S(1)}) fusion(bf16[7,7,1,384]{3,2,1,0:T(2,128)(2,1)} %bitcast.116, bf16[1,10,38,384]{3,2,1,0:T(8,128)(2,1)} %get-tuple-element.69), kind=kOutput, calls=%fused_computation.171 | convolution fusion | flops 4865920 | bytes 526592 | tf_op jit(solution)/shard_map/conv_general_dilated | solution.py:336
  82.2 0.9 multiply_reduce_fusion.1
  83.1 2.6 %fusion.46 = f32[1,7,7,384]{3,0,2,1:T(1,128)} fusion(bf16[1,10,38,384]{3,2,1,0:T(8,128)(2,1)S(1)} %copy-done.6, bf16[4,32,1,384]{3,1,0,2:T(8,128)(2,1)S(1)} %bitcast.104), kind=kOutput, calls=%fused_computation.57 | convolution fusion | flops 4816896 | bytes 465408 | tf_op jit(solution)/shard_map/conv_general_dilated | solution.py:336
  85.7 0.4 add_convert_fusion
  86.1 0.1 fusion.61
  86.2 0.4 copy-done.13
  86.6 1.8 %fusion.40 = f32[1,4,32,384]{3,0,2,1:T(1,128)S(1)} fusion(bf16[7,7,1,384]{3,2,1,0:T(2,128)(2,1)S(1)} %bitcast.119, bf16[1,10,38,384]{3,2,1,0:T(8,128)(2,1)S(1)} %fusion.61), kind=kOutput, calls=%fused_computation.49 | convolution fusion | flops 4816896 | bytes 526080 | tf_op jit(solution)/shard_map/conv_general_dilated | solution.py:336
  88.5 2.3 %collective-permute-start.4 = (bf16[4,32,384]{2,1,0:T(8,128)(2,1)S(1)}, bf16[4,32,384]{2,1,0:T(8,128)(2,1)}, u32[]{:S(2)}, u32[]{:S(2)}) collective-permute-start(bf16[4,32,384]{2,1,0:T(8,128)(2,1)S(1)} %fusion.68), channel_id=1, source_target_pairs={{0,16},{1,17},{2,18},{3,19},{4,20},{5,21},{6,22},{7,23},{8,24},{9,... | collective-permute-start | bytes 294920 | tf_op jit(solution)/shard_map/ppermute | solution.py:309
  90.8 1.3 collective-permute-start.5
  92.1 1.9 %select_select_fusion.1 = (bf16[128,1536]{1,0:T(8,128)(2,1)}, bf16[128,1536]{1,0:T(8,128)(2,1)}, f32[128,1536]{1,0:T(8,128)}) fusion(pred[]{:T(512)S(6)} %eq.9, pred[]{:T(512)S(6)} %eq.8, f32[128,1536]{1,0:T(8,128)S(1)} %convolution_add_fusion.1, f32[1536]{0:T(1024)S(1)} %copy-done.20, bf16[128,384]{1,0:T(8,128)(2,1)S(1)} %bitcast.115, ...), kind=kOutput, calls=%fused_computation.62 | convolution fusion | flops 155516928 | bytes 3643394 | tf_op jit(solution)/shard_map/dot_general | solution.py:374
  94.1 0.6 rsqrt.27
  94.7 0.6 div.36
  95.3 1.0 select_select_fusion.2
  96.4 0.0 copy-start.25
  96.4 0.0 copy-start.10
  96.4 2.8 %fusion.94 = (f32[128]{0:T(128)S(1)}, f32[128]{0:T(128)S(1)}, f32[128,384]{1,0:T(8,128)}) fusion(f32[128]{0:T(128)S(1)} %copy-done.24, f32[128]{0:T(128)} %div.36, f32[1,4,32,384]{3,2,0,1:T(8,128)S(1)} %copy.40, f32[384]{0:T(512)S(1)} %copy-done.16, bf16[384,1536]{1,0:T(8,128)(2,1)S(1)} %bitcast.107, bf16[128,384]{1,0:T(8,128)(2,1)S(1)} %bitcast.113, ...), kind=kOutput, calls=%fused_computation.163 | convolution fusion | flops 306020096 | bytes 3640832 | tf_op jit(solution)/shard_map/dot_general | solution.py:382
  99.2 1.1 multiply_convert_fusion.2
  100.3 1.3 collective-permute-start.7
  101.6 4.7 %collective-permute-start.6 = (bf16[3,32,384]{2,1,0:T(8,128)(2,1)S(1)}, bf16[3,32,384]{2,1,0:T(8,128)(2,1)S(1)}, u32[]{:S(2)}, u32[]{:S(2)}) collective-permute-start(bf16[3,32,384]{2,1,0:T(8,128)(2,1)S(1)} %bitcast.120), channel_id=1, source_target_pairs={{0,1},{1,2},{2,3},{3,4},{4,5},{5,6},{6,7},{7,8},{8,9},{9,10},{10,1... | collective-permute-start | bytes 221192 | tf_op jit(solution)/shard_map/ppermute | solution.py:297
  106.4 2.2 %fusion.74 = (f32[7,7,384]{2,1,0:T(8,128)S(1)}, bf16[1,7,7,384]{3,0,2,1:T(2,128)(2,1)S(1)}) fusion(pred[]{:T(512)S(6)} %eq.8, f32[1,7,7,384]{3,0,2,1:T(1,128)S(1)} %copy-done.10, pred[]{:T(512)S(6)} %eq.9, bf16[4,32,1,384]{3,1,0,2:T(8,128)(2,1)S(1)} %bitcast.102, bf16[1,10,38,384]{3,2,1,0:T(8,128)(2,1)S(1)} %copy-done.4), kind=kOutput, calls=%fused_computation.123 | convolution fusion | flops 4873344 | bytes 578306 | tf_op jit(solution)/shard_map/conv_general_dilated | solution.py:336
  108.6 0.0 copy-start.11
  108.6 0.2 fusion.76
  108.9 1.2 collective-permute-start.9
  110.2 0.1 collective-permute-start.8
  110.3 0.7 collective-permute-done.9
  111.0 0.1 fusion.60
  111.2 1.9 %fusion.38 = f32[1,4,32,384]{3,0,2,1:T(1,128)S(1)} fusion(bf16[7,7,1,384]{3,2,1,0:T(2,128)(2,1)S(1)} %bitcast.117, bf16[1,10,38,384]{3,2,1,0:T(8,128)(2,1)S(1)} %fusion.60), kind=kOutput, calls=%fused_computation.47 | convolution fusion | flops 4816896 | bytes 526080 | tf_op jit(solution)/shard_map/conv_general_dilated | solution.py:336
  113.1 0.7 select_bitcast_fusion.2
  113.8 0.3 copy-done.2
  114.1 0.6 convolution_multiply_fusion
  114.7 32.4 %sum_gradients.1 = (f32[96,384]{1,0:T(8,128)S(1)}, f32[64,384]{1,0:T(8,128)S(1)}) custom-call(f32[4,2,2,96,384]{4,3,2,1,0:T(8,128)S(1)} %bitcast.98, f32[64,384]{1,0:T(8,128)S(1)} %pad.25.dk), custom_call_target="tpu_custom_call" | custom-call | tf_op jit(solution)/shard_map/sum_gradients/pallas_call | solution.py:254
  147.1 0.7 copy.35
  147.9 0.7 copy.76
  (80 shorter events, 0.5 us)
Async XLA Ops:
  2.5 58.1 %collective-permute-start.1 = (bf16[2,3,32,384]{3,2,1,0:T(8,128)(2,1)S(1)}, bf16[2,3,32,384]{3,2,1,0:T(8,128)(2,1)S(1)}, u32[]{:S(2)}, u32[]{:S(2)}) collective-permute-start(bf16[2,3,32,384]{3,2,1,0:T(8,128)(2,1)S(1)} %get-tuple-element.51), channel_id=1, source_target_pairs={{1,0},{2,1},{3,2},{4,3},{5,4},{6,5},{7,6},{8,7},{9,8},{10,9},{11,1... | collective-permute-start | bytes 442376 | tf_op jit(solution)/shard_map/ppermute | solution.py:299
  3.8 56.8 %collective-permute-start = (bf16[2,3,32,384]{3,2,1,0:T(8,128)(2,1)S(1)}, bf16[2,3,32,384]{3,2,1,0:T(8,128)(2,1)S(1)}, u32[]{:S(2)}, u32[]{:S(2)}) collective-permute-start(bf16[2,3,32,384]{3,2,1,0:T(8,128)(2,1)S(1)} %get-tuple-element.50), channel_id=1, source_target_pairs={{0,1},{1,2},{2,3},{3,4},{4,5},{5,6},{6,7},{7,8},{8,9},{9,10},{10,1... | collective-permute-start | bytes 442376 | tf_op jit(solution)/shard_map/ppermute | solution.py:297
  53.2 2.4 %copy-start = (bf16[2,16,96,384]{3,2,1,0:T(8,128)(2,1)S(1)}, bf16[2,16,96,384]{3,2,1,0:T(8,128)(2,1)}, u32[]{:S(2)}) copy-start(bf16[2,16,96,384]{3,2,1,0:T(8,128)(2,1)} %get-tuple-element.8) | copy-start | bytes 7077892
  55.6 1.7 %copy-start.22 = (f32[1,2,384]{2,1,0:T(2,128)S(1)}, f32[1,2,384]{2,1,0:T(2,128)}, u32[]{:S(2)}) copy-start(f32[1,2,384]{2,1,0:T(2,128)} %param.21) | copy-start | bytes 9220
  55.6 1.7 %copy-start.23 = (f32[1,2,384]{2,1,0:T(2,128)S(1)}, f32[1,2,384]{2,1,0:T(2,128)}, u32[]{:S(2)}) copy-start(f32[1,2,384]{2,1,0:T(2,128)} %param.16) | copy-start | bytes 9220
  55.6 2.3 %copy-start.8 = (bf16[4,32,384]{2,1,0:T(8,128)(2,1)S(1)}, bf16[4,32,384]{2,1,0:T(8,128)(2,1)}, u32[]{:S(2)}) copy-start(bf16[4,32,384]{2,1,0:T(8,128)(2,1)} %param.14) | copy-start | bytes 294916
  55.6 2.3 %copy-start.9 = (bf16[4,32,384]{2,1,0:T(8,128)(2,1)S(1)}, bf16[4,32,384]{2,1,0:T(8,128)(2,1)}, u32[]{:S(2)}) copy-start(bf16[4,32,384]{2,1,0:T(8,128)(2,1)} %param.13) | copy-start | bytes 294916
  55.6 3.0 %copy-start.21 = (f32[1,2,384]{2,1,0:T(2,128)S(1)}, f32[1,2,384]{2,1,0:T(2,128)}, u32[]{:S(2)}) copy-start(f32[1,2,384]{2,1,0:T(2,128)} %param.17) | copy-start | bytes 9220
  55.6 3.6 %copy-start.14 = (f32[1,2,1536]{2,1,0:T(2,128)S(1)}, f32[1,2,1536]{2,1,0:T(2,128)}, u32[]{:S(2)}) copy-start(f32[1,2,1536]{2,1,0:T(2,128)} %param.19) | copy-start | bytes 36868
  55.6 4.2 %copy-start.7 = (bf16[1,2,49,384]{3,1,2,0:T(2,128)(2,1)S(1)}, bf16[1,2,49,384]{3,1,2,0:T(2,128)(2,1)}, u32[]{:S(2)}) copy-start(bf16[1,2,49,384]{3,1,2,0:T(2,128)(2,1)} %param.15) | copy-start | bytes 225796
  57.9 10.1 %copy-start.17 = (f32[384]{0:T(512)}, f32[384]{0:T(512)S(1)}, u32[]{:S(2)}) copy-start(f32[384]{0:T(512)S(1)} %get-tuple-element.67) | copy-start | bytes 4612
  60.6 1.1 copy-start.12
  61.6 4.2 %copy-start.5 = (bf16[1,10,38,384]{3,2,1,0:T(8,128)(2,1)}, bf16[1,10,38,384]{3,2,1,0:T(8,128)(2,1)S(1)}, u32[]{:S(2)}) copy-start(bf16[1,10,38,384]{3,2,1,0:T(8,128)(2,1)S(1)} %get-tuple-element.70) | copy-start | bytes 875524
  61.6 6.3 %copy-start.19 = (f32[384]{0:T(512)S(1)}, f32[384]{0:T(512)}, u32[]{:S(2)}) copy-start(f32[384]{0:T(512)} %get-tuple-element.33) | copy-start | bytes 4612
  68.7 2.9 %copy-start.26 = (f32[128]{0:T(128)S(1)}, f32[128]{0:T(128)}, u32[]{:S(2)}) copy-start(f32[128]{0:T(128)} %div.31) | copy-start | bytes 1540
  68.7 2.9 %copy-start.27 = (f32[128]{0:T(128)S(1)}, f32[128]{0:T(128)}, u32[]{:S(2)}) copy-start(f32[128]{0:T(128)} %rsqrt.25) | copy-start | bytes 1540
  72.7 13.4 %collective-permute-start.3 = (bf16[3,32,384]{2,1,0:T(8,128)(2,1)S(1)}, bf16[3,32,384]{2,1,0:T(8,128)(2,1)S(1)}, u32[]{:S(2)}, u32[]{:S(2)}) collective-permute-start(bf16[3,32,384]{2,1,0:T(8,128)(2,1)S(1)} %bitcast.123), channel_id=1, source_target_pairs={{1,0},{2,1},{3,2},{4,3},{5,4},{6,5},{7,6},{8,7},{9,8},{10,9},{11,1... | collective-permute-start | bytes 221192 | tf_op jit(solution)/shard_map/ppermute | solution.py:299
  74.0 12.1 %collective-permute-start.2 = (bf16[3,32,384]{2,1,0:T(8,128)(2,1)S(1)}, bf16[3,32,384]{2,1,0:T(8,128)(2,1)S(1)}, u32[]{:S(2)}, u32[]{:S(2)}) collective-permute-start(bf16[3,32,384]{2,1,0:T(8,128)(2,1)S(1)} %bitcast.122), channel_id=1, source_target_pairs={{0,1},{1,2},{2,3},{3,4},{4,5},{5,6},{6,7},{7,8},{8,9},{9,10},{10,1... | collective-permute-start | bytes 221192 | tf_op jit(solution)/shard_map/ppermute | solution.py:297
  78.5 4.6 %copy-start.6 = (bf16[1,10,38,384]{3,2,1,0:T(8,128)(2,1)S(1)}, bf16[1,10,38,384]{3,2,1,0:T(8,128)(2,1)}, u32[]{:S(2)}) copy-start(bf16[1,10,38,384]{3,2,1,0:T(8,128)(2,1)} %copy-done.5) | copy-start | bytes 875524
  83.1 2.6 %copy-start.15 = (f32[384]{0:T(512)S(1)}, f32[384]{0:T(512)}, u32[]{:S(2)}) copy-start(f32[384]{0:T(512)} %get-tuple-element.68) | copy-start | bytes 4612
  83.1 2.6 %copy-start.18 = (f32[384]{0:T(512)S(1)}, f32[384]{0:T(512)}, u32[]{:S(2)}) copy-start(f32[384]{0:T(512)} %get-tuple-element.32) | copy-start | bytes 4612
  85.7 0.9 copy-start.13
  86.6 5.5 %copy-start.20 = (f32[1536]{0:T(1024)S(1)}, f32[1536]{0:T(1024)}, u32[]{:S(2)}) copy-start(f32[1536]{0:T(1024)} %get-tuple-element.28) | copy-start | bytes 18436
  88.5 6.8 %collective-permute-start.4 = (bf16[4,32,384]{2,1,0:T(8,128)(2,1)S(1)}, bf16[4,32,384]{2,1,0:T(8,128)(2,1)}, u32[]{:S(2)}, u32[]{:S(2)}) collective-permute-start(bf16[4,32,384]{2,1,0:T(8,128)(2,1)S(1)} %fusion.68), channel_id=1, source_target_pairs={{0,16},{1,17},{2,18},{3,19},{4,20},{5,21},{6,22},{7,23},{8,24},{9,... | collective-permute-start | bytes 294920 | tf_op jit(solution)/shard_map/ppermute | solution.py:309
  90.8 4.5 %collective-permute-start.5 = (bf16[4,32,384]{2,1,0:T(8,128)(2,1)S(1)}, bf16[4,32,384]{2,1,0:T(8,128)(2,1)}, u32[]{:S(2)}, u32[]{:S(2)}) collective-permute-start(bf16[4,32,384]{2,1,0:T(8,128)(2,1)S(1)} %fusion.68), channel_id=1, source_target_pairs={{16,0},{17,1},{18,2},{19,3},{20,4},{21,5},{22,6},{23,7},{24,8},{25... | collective-permute-start | bytes 294920 | tf_op jit(solution)/shard_map/ppermute | solution.py:309
  94.1 2.3 %copy-start.1 = (bf16[1,16,96,384]{3,2,1,0:T(8,128)(2,1)S(1)}, bf16[1,16,96,384]{3,2,1,0:T(8,128)(2,1)}, u32[]{:S(2)}) copy-start(bf16[1,16,96,384]{3,2,1,0:T(8,128)(2,1)} %get-tuple-element.40) | copy-start | bytes 3538948
  94.7 1.7 %copy-start.16 = (f32[384]{0:T(512)S(1)}, f32[384]{0:T(512)}, u32[]{:S(2)}) copy-start(f32[384]{0:T(512)} %get-tuple-element.68) | copy-start | bytes 4612
  95.2 1.1 copy-start.24
  96.4 2.8 %copy-start.25 = (f32[128]{0:T(128)S(1)}, f32[128]{0:T(128)}, u32[]{:S(2)}) copy-start(f32[128]{0:T(128)} %div.36) | copy-start | bytes 1540
  96.4 9.9 %copy-start.4 = (bf16[1,10,38,384]{3,2,1,0:T(8,128)(2,1)S(1)}, bf16[1,10,38,384]{3,2,1,0:T(8,128)(2,1)}, u32[]{:S(2)}) copy-start(bf16[1,10,38,384]{3,2,1,0:T(8,128)(2,1)} %get-tuple-element.69) | copy-start | bytes 875524
  96.4 9.9 %copy-start.10 = (f32[1,7,7,384]{3,0,2,1:T(1,128)S(1)}, f32[1,7,7,384]{3,0,2,1:T(1,128)}, u32[]{:S(2)}) copy-start(f32[1,7,7,384]{3,0,2,1:T(1,128)} %fusion.46) | copy-start | bytes 225796
  100.3 10.7 %collective-permute-start.7 = (bf16[3,32,384]{2,1,0:T(8,128)(2,1)S(1)}, bf16[3,32,384]{2,1,0:T(8,128)(2,1)S(1)}, u32[]{:S(2)}, u32[]{:S(2)}) collective-permute-start(bf16[3,32,384]{2,1,0:T(8,128)(2,1)S(1)} %bitcast.121), channel_id=1, source_target_pairs={{1,0},{2,1},{3,2},{4,3},{5,4},{6,5},{7,6},{8,7},{9,8},{10,9},{11,1... | collective-permute-start | bytes 221192 | tf_op jit(solution)/shard_map/ppermute | solution.py:299
  101.6 9.4 %collective-permute-start.6 = (bf16[3,32,384]{2,1,0:T(8,128)(2,1)S(1)}, bf16[3,32,384]{2,1,0:T(8,128)(2,1)S(1)}, u32[]{:S(2)}, u32[]{:S(2)}) collective-permute-start(bf16[3,32,384]{2,1,0:T(8,128)(2,1)S(1)} %bitcast.120), channel_id=1, source_target_pairs={{0,1},{1,2},{2,3},{3,4},{4,5},{5,6},{6,7},{7,8},{8,9},{9,10},{10,1... | collective-permute-start | bytes 221192 | tf_op jit(solution)/shard_map/ppermute | solution.py:297
  106.3 3.8 %copy-start.3 = (bf16[128,1536]{1,0:T(8,128)(2,1)S(1)}, bf16[128,1536]{1,0:T(8,128)(2,1)}, u32[]{:S(2)}) copy-start(bf16[128,1536]{1,0:T(8,128)(2,1)} %get-tuple-element.45) | copy-start | bytes 1179652
  108.6 2.6 %copy-start.11 = (bf16[1,1,49,384]{3,1,2,0:T(2,128)(2,1)S(1)}, bf16[1,1,49,384]{3,1,2,0:T(2,128)(2,1)}, u32[]{:S(2)}) copy-start(bf16[1,1,49,384]{3,1,2,0:T(2,128)(2,1)} %get-tuple-element.56) | copy-start | bytes 112900
  108.9 2.1 %collective-permute-start.9 = (bf16[49,384]{1,0:T(8,128)(2,1)S(1)}, bf16[49,384]{1,0:T(8,128)(2,1)S(1)}, u32[]{:S(2)}, u32[]{:S(2)}) collective-permute-start(bf16[49,384]{1,0:T(8,128)(2,1)S(1)} %convert_element_type.137), channel_id=1, source_target_pairs={{0,16},{16,0},{1,17},{17,1},{2,18},{18,2},{3,19},{19,3},{4,20},{20... | collective-permute-start | bytes 112904 | tf_op jit(solution)/shard_map/ppermute | solution.py:323
  110.2 3.6 %collective-permute-start.8 = (bf16[128,1920]{1,0:T(8,128)(2,1)S(1)}, bf16[128,1920]{1,0:T(8,128)(2,1)S(1)}, u32[]{:S(2)}, u32[]{:S(2)}) collective-permute-start(bf16[128,1920]{1,0:T(8,128)(2,1)S(1)} %pad_maximum_fusion.1), channel_id=1, source_target_pairs={{0,16},{16,0},{1,17},{17,1},{2,18},{18,2},{3,19},{19,3},{4,20},{20... | collective-permute-start | bytes 1474568 | tf_op jit(solution)/shard_map/ppermute | solution.py:323
  113.1 1.1 copy-start.2

commit v2 on v1

--- a/solution.py
+++ b/solution.py
@@ -14,84 +14,159 @@
 MESH = pl.DeviceIdType.MESH
 
 
-def turned(q):
-    return q + (q // 2) * (1 - 2 * (q % 2))
-
-
-def chip_at(k):
-    q = k // 4
-    r = k % 4
-    odd = q % 2
-    z = r + odd * (3 - 2 * r)
-    return z * 4 + turned(q)
-
-
-def place_of(p):
-    z = p // 4
-    q = turned(p % 4)
-    odd = q % 2
-    return q * 4 + z + odd * (3 - 2 * z)
-
-
 def gather_kernel(
-    n, win, wout, win_all, wout_all, own_sem, send_sem, recv_sem, over_send, over_recv
+    win,
+    wout,
+    x,
+    win_all,
+    wout_all,
+    above,
+    below,
+    own_sem,
+    z_send,
+    z_recv,
+    one_send,
+    one_recv,
+    two_send,
+    two_recv,
+    over_send,
+    over_recv,
+    rim_send,
+    rim_recv,
 ):
     core = lax.axis_index("segment")
     p = lax.axis_index("space")
-    k = place_of(p)
-    ways = (chip_at((k + 1) % n), chip_at((k + n - 1) % n))
+    z = p // 4
+    y = (p // 2) % 2
+    xx = p % 2
+    after, before = (core, (p + 1) % 16), (core, (p + 15) % 16)
+    over_x = (core, z * 4 + y * 2 + 1 - xx)
+    over_y = (core, z * 4 + (1 - y) * 2 + xx)
+    over_z = {j: (core, ((z + j) % 4) * 4 + y * 2 + xx) for j in (1, 2, 3)}
+    other_core = (1 - core, p)
     barrier = pltpu.get_barrier_semaphore()
-    for device in ((core, ways[0]), (core, ways[1]), (1 - core, p)):
+    greeted = [over_x, over_y, other_core, after, before] + list(over_z.values())
+    for device in greeted:
         pl.semaphore_signal(barrier, inc=1, device_id=device, device_id_type=MESH)
-    pl.semaphore_wait(barrier, 3)
-
-    half = n // 2
-    steps = [
-        (t, b, d) for t in range(half) for b in (1, 0) for d in (0, 1) if t < half - 1 or b != d
-    ]
-
-    def carry(mine, mine_all, other_all, mine_slot):
-        def hop(t, b, d):
-            origin = chip_at((k + (n - t if d == 0 else t)) % n)
+    pl.semaphore_wait(barrier, len(greeted))
+
+    def remote(src, dst, send, recv, device):
+        return pltpu.make_async_remote_copy(
+            src_ref=src,
+            dst_ref=dst,
+            send_sem=send,
+            recv_sem=recv,
+            device_id=device,
+            device_id_type=MESH,
+        )
+
+    width, rows = above.shape[1], x.shape[1]
+    rims = []
+    for m in (0, 1):
+        rims.append(
+            remote(
+                x.at[m, pl.ds(rows - width, width)],
+                above.at[m],
+                rim_send.at[m, 0],
+                rim_recv.at[m, 0],
+                after,
+            )
+        )
+        rims.append(
+            remote(
+                x.at[m, pl.ds(0, width)], below.at[m], rim_send.at[m, 1], rim_recv.at[m, 1], before
+            )
+        )
+
+    def carry(mine, mine_all, other_all, slot):
+        def cell(j, turned_y, turned_x):
+            yy = 1 - y if turned_y else y
+            xo = 1 - xx if turned_x else xx
+            return ((z + 4 - j) % 4) * 4 + yy * 2 + xo
+
+        def first(b):
+            return (over_x, 0, 1) if b == 1 else (over_y, 1, 0)
+
+        def second(b):
+            return (over_y, 1, 0) if b == 1 else (over_x, 0, 1)
+
+        pending = []
+
+        def start(copy):
+            copy.start()
+            pending.append(copy)
+
+        arrivals = []
+
+        def across(origin, b, number):
+            start(
+                remote(
+                    mine_all.at[b, origin],
+                    mine_all.at[b, origin],
+                    over_send.at[number, b],
+                    over_recv.at[number, b],
+                    other_core,
+                )
+            )
+            arrivals.append((other_all.at[b, origin], over_recv.at[number, b]))
+
+        def landed(ref, sem):
+            pltpu.make_async_copy(ref, ref, sem).wait()
+
+        def line(j, b):
+            origin = cell(j, 0, 0)
             spot = mine_all.at[b, origin]
-            return pltpu.make_async_remote_copy(
-                src_ref=mine.at[mine_slot(b)] if t == 0 else spot,
-                dst_ref=spot,
-                send_sem=send_sem.at[t, b, d],
-                recv_sem=recv_sem.at[t, b, d],
-                device_id=(core, ways[d]),
-                device_id_type=MESH,
-            )
-
-        def arrival(t, b, d):
-            origin = chip_at((k + (n - t - 1 if d == 0 else t + 1)) % n)
-            return mine_all.at[b, origin], other_all.at[b, origin]
-
-        def across(t, b, d):
-            spot, _ = arrival(t, b, d)
-            return pltpu.make_async_remote_copy(
-                src_ref=spot,
-                dst_ref=spot,
-                send_sem=over_send.at[t, b, d],
-                recv_sem=over_recv.at[t, b, d],
-                device_id=(1 - core, p),
-                device_id_type=MESH,
-            )
+            if j:
+                landed(spot, z_recv.at[j, b])
+            src = spot if j else mine.at[slot(b)]
+            start(remote(src, spot, one_send.at[j, b], one_recv.at[j, b], first(b)[0]))
+            start(remote(src, spot, two_send.at[j, b, 0], two_recv.at[j, b, 0], second(b)[0]))
+            if j:
+                across(origin, b, j)
+
+        def once(j, b):
+            _, ty, tx = first(b)
+            origin = cell(j, ty, tx)
+            spot = mine_all.at[b, origin]
+            landed(spot, one_recv.at[j, b])
+            start(remote(spot, spot, two_send.at[j, b, 1], two_recv.at[j, b, 1], second(b)[0]))
+            across(origin, b, 4 + j)
+
+        def twice(j, b):
+            _, ty, tx = second(b)
+            for which, origin in enumerate((cell(j, ty, tx), cell(j, 1, 1))):
+                landed(mine_all.at[b, origin], two_recv.at[j, b, which])
+                across(origin, b, 8 + 2 * j + which)
 
         for b in (1, 0):
-            for d in (0, 1):
-                hop(0, b, d).start()
-        for t, b, d in steps:
-            spot, _ = arrival(t, b, d)
-            pltpu.make_async_copy(spot, spot, recv_sem.at[t, b, d]).wait()
-            if (t + 1, b, d) in steps:
-                hop(t + 1, b, d).start()
-            across(t, b, d).start()
-        for t, b, d in steps:
-            hop(t, b, d).wait_send()
-            across(t, b, d).wait_send()
-            _, other = arrival(t, b, d)
-            pltpu.make_async_copy(other, other, over_recv.at[t, b, d]).wait()
+            line(0, b)
+        for j in (1, 3, 2):
+            for b in (1, 0):
+                spot = mine_all.at[b, p]
+                start(remote(mine.at[slot(b)], spot, z_send.at[j, b], z_recv.at[j, b], over_z[j]))
+        for c in rims:
+            c.start()
+        for act, j in (
+            (once, 0),
+            (line, 1),
+            (line, 3),
+            (once, 1),
+            (twice, 0),
+            (line, 2),
+            (once, 3),
+            (twice, 1),
+            (once, 2),
+            (twice, 3),
+            (twice, 2),
+        ):
+            for b in (1, 0):
+                act(j, b)
+        for c in rims:
+            c.wait()
+        for ref, sem in arrivals:
+            landed(ref, sem)
+        for c in pending:
+            c.wait_send()
 
     def own(slot):
         copies = []
@@ -119,26 +194,100 @@
             c.wait()
 
 
-def gathered(w_in, w_out):
+def gathered(w_in, w_out, x, width):
     n = lax.axis_size("space")
+    p = lax.axis_index("space")
     win, wout = w_in[0], w_out[0]
-    sems = pltpu.SemaphoreType.DMA((n // 2, 2, 2))
-    win_all, wout_all = pl.pallas_call(
-        functools.partial(gather_kernel, n),
+    dma = pltpu.SemaphoreType.DMA
+    rim = jax.ShapeDtypeStruct((2, width) + x.shape[2:], x.dtype)
+    win_all, wout_all, above, below = pl.pallas_call(
+        gather_kernel,
         out_shape=(
             jax.ShapeDtypeStruct((2, n) + win.shape[1:], win.dtype),
             jax.ShapeDtypeStruct((2, n) + wout.shape[1:], wout.dtype),
+            rim,
+            rim,
         ),
-        in_specs=[pl.BlockSpec(memory_space=pl.ANY)] * 2,
-        out_specs=(pl.BlockSpec(memory_space=pl.ANY),) * 2,
-        scratch_shapes=[pltpu.SemaphoreType.DMA((2, 2)), sems, sems, sems, sems],
+        in_specs=[pl.BlockSpec(memory_space=pl.ANY)] * 3,
+        out_specs=(pl.BlockSpec(memory_space=pl.ANY),) * 4,
+        scratch_shapes=[
+            dma((2, 2)),
+            dma((4, 2)),
+            dma((4, 2)),
+            dma((4, 2)),
+            dma((4, 2)),
+            dma((4, 2, 2)),
+            dma((4, 2, 2)),
+            dma((16, 2)),
+            dma((16, 2)),
+            dma((2, 2)),
+            dma((2, 2)),
+        ],
         compiler_params=pltpu.CompilerParams(collective_id=0, has_side_effects=True),
         name="gather_weights",
-    )(win, wout)
+    )(win, wout, x)
+    above = jnp.where(p == 0, jnp.zeros_like(above), above)
+    below = jnp.where(p == n - 1, jnp.zeros_like(below), below)
     return (
         win_all.reshape(2, n * win.shape[1], win.shape[2]),
         wout_all.reshape(2, n * wout.shape[1], wout.shape[2]),
+        jnp.concatenate([above, x, below], axis=1),
     )
+
+
+def rim_kernel(n, du, out, send_sem, recv_sem):
+    core = lax.axis_index("segment")
+    p = lax.axis_index("space")
+    after, before = (core, (p + 1) % n), (core, (p + n - 1) % n)
+    rows = du.shape[0]
+    width = (out.shape[0] - rows) // 2
+    barrier = pltpu.get_barrier_semaphore()
+    for device in (after, before):
+        pl.semaphore_signal(barrier, inc=1, device_id=device, device_id_type=MESH)
+    pl.semaphore_wait(barrier, 2)
+    top, bottom = pl.ds(0, width), pl.ds(width + rows, width)
+    down = pltpu.make_async_remote_copy(
+        src_ref=du.at[pl.ds(rows - width, width)],
+        dst_ref=out.at[top],
+        send_sem=send_sem.at[0],
+        recv_sem=recv_sem.at[0],
+        device_id=after,
+        device_id_type=MESH,
+    )
+    up = pltpu.make_async_remote_copy(
+        src_ref=du.at[top],
+        dst_ref=out.at[bottom],
+        send_sem=send_sem.at[1],
+        recv_sem=recv_sem.at[1],
+        device_id=before,
+        device_id_type=MESH,
+    )
+    down.start()
+    up.start()
+    out[pl.ds(width, rows)] = du[...]
+    down.wait()
+    up.wait()
+
+    @pl.when(p == 0)
+    def _():
+        out[top] = jnp.zeros((width,) + du.shape[1:], out.dtype)
+
+    @pl.when(p == n - 1)
+    def _():
+        out[bottom] = jnp.zeros((width,) + du.shape[1:], out.dtype)
+
+
+def rimmed_by_kernel(du, width):
+    n = lax.axis_size("space")
+    return pl.pallas_call(
+        functools.partial(rim_kernel, n),
+        out_shape=jax.ShapeDtypeStruct((du.shape[0] + 2 * width,) + du.shape[1:], du.dtype),
+        in_specs=[pl.BlockSpec(memory_space=pltpu.VMEM)],
+        out_specs=pl.BlockSpec(memory_space=pltpu.VMEM),
+        scratch_shapes=[pltpu.SemaphoreType.DMA((2,)), pltpu.SemaphoreType.DMA((2,))],
+        compiler_params=pltpu.CompilerParams(collective_id=2, has_side_effects=True),
+        name="gradient_rims",
+    )(du)
 
 
 def sum_kernel(
@@ -408,15 +557,16 @@
     norm = 1.0 / math.sqrt(2.0 * rows * lax.axis_size("space") * cols)
     paired = segments == 2 and lax.axis_size("space") == 16
     if paired:
-        w_in_all, w_out_all = gathered(w_in, w_out)
+        w_in_all, w_out_all, rimmed_both = gathered(
+            w_in, w_out, jnp.concatenate([stash_down, stash_up]), half
+        )
     else:
         w_in_all, w_out_all = (
             lax.all_gather(w_in, "space", axis=2, tiled=True)[0],
             lax.all_gather(w_out, "space", axis=2, tiled=True)[0],
         )
-    x_down = stash_down[0]
-    x_up = stash_up[0]
-    rimmed_both = padded_2(jnp.stack([x_down, x_up]), (("space", 1),), half)
+        both = jnp.concatenate([stash_down, stash_up])
+        rimmed_both = padded_2(both, (("space", 1),), half)
     down_in = grad_down
     up_in = grad_up
     out_down = jnp.zeros_like(grad_down)
@@ -468,7 +618,10 @@
             )
 
         du, hidden, outer = front_live() if paired else lax.cond(active, front_live, front_spare)
-        du_rimmed = padded_2(du, (("space", 0),), half)
+        if paired:
+            du_rimmed = rimmed_by_kernel(du, half)
+        else:
+            du_rimmed = padded_2(du, (("space", 0),), half)
 
         def back_live():
             du_pad = jnp.pad(du_rimmed.astype(jnp.float32), ((0, 0), (half, half), (0, 0)))
@@ -491,7 +644,9 @@
         hid_up = jnp.where(on_up, hidden, hid_up)
         outer_down = jnp.where(on_down, outer, outer_down)
         outer_up = jnp.where(on_up, outer, outer_up)
-        if step + 1 < segments:
+        if paired and step == 0:
+            down_in = up_in = swapped(dx, "segment", 0)
+        elif step + 1 < segments:
             down_in = passed_along(dx, "segment", -1)
             up_in = passed_along(dx, "segment", 1)
     levels = segments.bit_length() - 1

time: 149 us -> 138 us (0.926)
  starting transfers between devices: 23.6 us -> 0.14 us
  Pallas kernels: 76.3 us -> 83.9 us
  other arithmetic: 7.77 us -> 11.2 us
  local copies, waits for them, and re-layouts: 14 us -> 15.8 us
    ppermute x8 -> x0, starting transfers between devices: 22.2 us -> none  [the longest x3 14.8 us: padded_2(): lax.ppermute(tail, axis, [(i, (i + 1) % count) for i in range(ends)])]
    pallas_call x1 -> x3, Pallas kernels: 43.9 us -> 56.3 us  [the longest x1 36.5 us: gathered(): pl.pallas_call(gather_kernel, out_shape=(jax.ShapeDtypeStruct((2, n) + wi...]
    pallas_call x1, Pallas kernels: 32.4 us -> 27.6 us  [summed(): pl.pallas_call(sum_kernel, out_shape=(jax.ShapeDtypeStruct((share, chans)...]
    unnamed x63 -> x77, local copies, waits for them, and re-layouts: 3.54 us -> 6.07 us
  transfers between devices with their start and end apart: 10 -> 3, of which waited for: 1 -> 0; matrix products, arithmetic and copies ran while one was open for 15% -> 10% of each run, Pallas kernels for 30% -> 0%
where the time goes in v2:
time: 138 us; the launch traced here: 137 us
  Pallas kernels  83.9 us (61%)
  matrix products  24.8 us (18%)
  local copies, waits for them, and re-layouts  15.8 us (11%)
  other arithmetic  11.2 us (8%)
    pallas_call x1, Pallas kernels, gathered(): pl.pallas_call(gather_kernel, out_shape=(jax.ShapeDtypeStruct((2, n) + wi...  36.5 us
    pallas_call x1, Pallas kernels, summed(): pl.pallas_call(sum_kernel, out_shape=(jax.ShapeDtypeStruct((share, chans)...  27.6 us
    pallas_call x2, Pallas kernels, rimmed_by_kernel(): pl.pallas_call(functools.partial(rim_kernel, n), out_shape=jax.ShapeDtype...  19.7 us
    conv_general_dilated x6, matrix products, grouped_conv(): lax.conv_general_dilated(padded[None], filters, (1, 1), 'VALID', dimensio...  16.9 us
    unnamed x77, local copies, waits for them, and re-layouts  6.07 us
    dot_general x2, matrix products, pointwise_back(): lax.dot_general(da, w_first, (((1,), (1,)), ((), ())), preferred_element_...  4.98 us
  transfers between devices with their start and end apart: 3, of which 0 were waited for; matrix products, arithmetic and copies ran while one was open for 10% of the time, Pallas kernels for 0%

profile of v2, /device:TPU:0, one launch (start us, length us, event | category | flops | bytes accessed | tf_op | source)
XLA Modules:
  0.0 137.1 jit_solution(1558614744383613418)
XLA Ops:
  0.6 0.9 constant_dynamic-update-slice_fusion.1
  1.6 0.9 constant_dynamic-update-slice_fusion.x
  2.5 0.7 copy-done.4
  3.1 36.5 %gather_weights.1 = (bf16[2,16,24,1536]{3,2,1,0:T(8,128)(2,1)}, bf16[2,16,96,384]{3,2,1,0:T(8,128)(2,1)}, bf16[2,3,32,384]{3,2,1,0:T(8,128)(2,1)}, bf16[2,3,32,384]{3,2,1,0:T(8,128)(2,1)}) custom-call(bf16[2,24,1536]{2,1,0:T(8,128)(2,1)} %bitcast.107, bf16[2,96,384]{2,1,0:T(8,128)(2,1)} %bitcast.108, bf16[2,4,32,384]{3,2,1,0:T(8,128)(2,1)} %copy-done.4), custom_call_target="tpu_custom_call" | custom-call | tf_op jit(solution)/shard_map/gather_weights/pallas_call | solution.py:203
  39.7 1.0 broadcast_select_fusion.4
  40.6 0.0 copy-start.16
  40.6 1.0 pad_maximum_fusion
  41.7 0.8 select_bitcast_fusion
  42.4 0.1 pad_bitcast_fusion.3
  42.5 0.8 constant_dynamic-slice_fusion.3
  43.3 4.1 %fusion.94 = (f32[4,32]{1,0:T(4,128)S(1)}, f32[1,4,32,384]{3,0,2,1:T(1,128)S(1)}) fusion(bf16[7,7,1,384]{3,2,1,0:T(2,128)(2,1)S(1)} %bitcast.114, bf16[1,10,38,384]{3,2,1,0:T(8,128)(2,1)S(1)} %pad_bitcast_fusion.3), kind=kOutput, calls=%fused_computation.160 | convolution fusion | flops 4865920 | bytes 526592 | tf_op jit(solution)/shard_map/conv_general_dilated | solution.py:485
  47.5 0.6 div.31
  48.1 0.9 multiply_reduce_fusion.3
  49.0 0.7 copy.34
  49.7 0.6 rsqrt.25
  50.4 1.2 fusion.93
  51.6 0.9 copy-done
  52.5 0.0 copy-start.24
  52.5 0.0 copy-start.17
  52.5 0.0 copy-start.18
  52.5 1.3 fusion.92
  53.8 0.6 fusion.78
  54.4 0.6 fusion.76
  55.0 0.6 copy-done.26
  55.6 0.4 add_convert_fusion.1
  56.0 0.6 dynamic-slice_reduce_fusion
  56.6 0.7 multiply_convert_fusion.5
  57.3 0.4 convolution_add_fusion.1
  57.7 2.9 %fusion.91 = (f32[128]{0:T(128)S(1)}, f32[128]{0:T(128)S(1)}, f32[128,384]{1,0:T(8,128)}) fusion(f32[128]{0:T(128)} %rsqrt.25, f32[128]{0:T(128)S(1)} %copy-done.33, f32[1,4,32,384]{3,2,0,1:T(8,128)S(1)} %copy-done.7, f32[384]{0:T(512)S(1)} %copy-done.27, bf16[384,1536]{1,0:T(8,128)(2,1)S(1)} %bitcast.97, bf16[128,384]{1,0:T(8,128)(2,1)} %bitcast.110, ...), kind=kOutput, calls=%fused_computation.157 | convolution fusion | flops 306020096 | bytes 3640832 | tf_op jit(solution)/shard_map/dot_general | solution.py:531
  60.6 1.7 %multiply_convert_fusion.4 = bf16[128,384]{1,0:T(8,128)(2,1)} fusion(f32[128,384]{1,0:T(8,128)} %get-tuple-element.54, f32[1,4,32,384]{3,2,0,1:T(8,128)S(1)} %copy-done.7, f32[128]{0:T(128)S(1)} %broadcast_multiply_fusion.4, f32[128]{0:T(128)S(1)} %copy-done.33, f32[128]{0:T(128)S(1)} %broadcast_multiply_fusion.5, f32[128]{0:T(128)S(1)} %copy-done.34), kind=kLoop, calls=%fused_computation.98 | loop fusion | flops 344064 | bytes 493568 | tf_op jit(solution)/shard_map/convert_element_type | solution.py:536
  62.3 9.8 %gradient_rims.2 = bf16[10,32,384]{2,1,0:T(8,128)(2,1)} custom-call(bf16[4,32,384]{2,1,0:T(8,128)(2,1)} %bitcast.103), custom_call_target="tpu_custom_call" | custom-call | tf_op jit(solution)/shard_map/gradient_rims/pallas_call | solution.py:282
  72.2 1.0 pad_bitcast_fusion.2
  73.2 0.0 copy-start.20
  73.2 1.9 %fusion.39 = f32[1,4,32,384]{3,0,2,1:T(1,128)S(1)} fusion(bf16[7,7,1,384]{3,2,1,0:T(2,128)(2,1)S(1)} %bitcast.115, bf16[1,10,38,384]{3,2,1,0:T(8,128)(2,1)S(1)} %pad_bitcast_fusion.2), kind=kOutput, calls=%fused_computation.46 | convolution fusion | flops 4816896 | bytes 526080 | tf_op jit(solution)/shard_map/conv_general_dilated | solution.py:485
  75.1 0.7 fusion.64
  75.8 0.1 pad_bitcast_fusion.1
  75.9 0.0 copy-start.10
  75.9 4.1 %fusion.95 = (f32[4,32]{1,0:T(4,128)S(1)}, f32[1,4,32,384]{3,0,2,1:T(1,128)S(1)}) fusion(bf16[7,7,1,384]{3,2,1,0:T(2,128)(2,1)S(1)} %bitcast.112, bf16[1,10,38,384]{3,2,1,0:T(8,128)(2,1)S(1)} %pad_bitcast_fusion.1), kind=kOutput, calls=%fused_computation.161 | convolution fusion | flops 4865920 | bytes 526592 | tf_op jit(solution)/shard_map/conv_general_dilated | solution.py:485
  80.1 0.9 multiply_reduce_fusion.1
  81.0 0.4 add_convert_fusion
  81.5 2.6 %fusion.45 = f32[1,7,7,384]{3,0,2,1:T(1,128)} fusion(bf16[1,10,38,384]{3,2,1,0:T(8,128)(2,1)S(1)} %copy-done.13, bf16[4,32,1,384]{3,1,0,2:T(8,128)(2,1)S(1)} %bitcast.104), kind=kOutput, calls=%fused_computation.54 | convolution fusion | flops 4816896 | bytes 465408 | tf_op jit(solution)/shard_map/conv_general_dilated | solution.py:485
  84.1 2.0 %select_select_fusion.1 = (bf16[128,1536]{1,0:T(8,128)(2,1)}, bf16[128,1536]{1,0:T(8,128)(2,1)}, f32[128,1536]{1,0:T(8,128)}) fusion(pred[]{:T(512)S(6)} %eq.17, pred[]{:T(512)S(6)} %eq.14, f32[128,1536]{1,0:T(8,128)S(1)} %convolution_add_fusion.1, f32[1536]{0:T(1024)S(1)} %copy-done.29, bf16[128,384]{1,0:T(8,128)(2,1)S(1)} %bitcast.111, ...), kind=kOutput, calls=%fused_computation.59 | convolution fusion | flops 155516928 | bytes 3643394 | tf_op jit(solution)/shard_map/dot_general | solution.py:523
  86.0 0.1 rsqrt.27
  86.1 0.1 div.36
  86.2 2.1 %fusion.90 = (f32[128]{0:T(128)S(1)}, f32[128]{0:T(128)S(1)}, f32[128,384]{1,0:T(8,128)S(1)}) fusion(f32[128]{0:T(128)S(1)} %rsqrt.27, f32[128]{0:T(128)S(1)} %div.36, f32[1,4,32,384]{3,2,0,1:T(8,128)S(1)} %copy.37, f32[384]{0:T(512)} %get-tuple-element.64, bf16[384,1536]{1,0:T(8,128)(2,1)S(1)} %bitcast.99, bf16[128,384]{1,0:T(8,128)(2,1)S(1)} %bitcast.109, ...), kind=kOutput, calls=%fused_computation.156 | convolution fusion | flops 306020096 | bytes 3640832 | tf_op jit(solution)/shard_map/dot_general | solution.py:531
  88.4 0.0 copy-start.21
  88.4 0.8 multiply_convert_fusion.2
  89.2 9.9 %gradient_rims.3 = bf16[10,32,384]{2,1,0:T(8,128)(2,1)} custom-call(bf16[4,32,384]{2,1,0:T(8,128)(2,1)} %bitcast.105), custom_call_target="tpu_custom_call" | custom-call | tf_op jit(solution)/shard_map/gradient_rims/pallas_call | solution.py:282
  99.1 1.0 pad_bitcast_fusion
  100.1 1.9 %fusion.37 = f32[1,4,32,384]{3,0,2,1:T(1,128)S(1)} fusion(bf16[7,7,1,384]{3,2,1,0:T(2,128)(2,1)S(1)} %bitcast.113, bf16[1,10,38,384]{3,2,1,0:T(8,128)(2,1)S(1)} %pad_bitcast_fusion), kind=kOutput, calls=%fused_computation.44 | convolution fusion | flops 4816896 | bytes 526080 | tf_op jit(solution)/shard_map/conv_general_dilated | solution.py:485
  102.1 0.0 copy-start.11
  102.1 0.1 select_select_fusion.2
  102.2 0.1 collective-permute-start.1
  102.3 0.7 copy-done.11
  103.0 0.1 copy-done.15
  103.1 0.0 copy-done.19
  103.1 2.2 %fusion.70 = (f32[7,7,384]{2,1,0:T(8,128)S(1)}, bf16[1,7,7,384]{3,0,2,1:T(2,128)(2,1)S(1)}) fusion(pred[]{:T(512)S(6)} %eq.14, f32[1,7,7,384]{3,0,2,1:T(1,128)S(1)} %copy-done.19, pred[]{:T(512)S(6)} %eq.17, bf16[4,32,1,384]{3,1,0,2:T(8,128)(2,1)S(1)} %bitcast.106, bf16[1,10,38,384]{3,2,1,0:T(8,128)(2,1)S(1)} %copy-done.15), kind=kOutput, calls=%fused_computation.116 | convolution fusion | flops 4873344 | bytes 578306 | tf_op jit(solution)/shard_map/conv_general_dilated | solution.py:485
  105.3 0.2 fusion.72
  105.6 0.1 collective-permute-start.2
  105.7 1.6 %select_bitcast_fusion.2 = (bf16[1,4,32,384]{3,2,1,0:T(8,128)(2,1)}, bf16[1,4,32,384]{3,2,1,0:T(8,128)(2,1)}) fusion(bf16[4,32,384]{2,1,0:T(8,128)(2,1)} %fusion.64, pred[]{:T(512)S(6)} %eq.17, pred[]{:T(512)S(6)} %eq.14, f32[1,4,32,384]{3,0,2,1:T(1,128)S(1)} %fusion.37, bf16[4,32,384]{2,1,0:T(8,128)(2,1)S(1)} %collective-permute-done), kind=kLoop, calls=%fused_computation.111 | loop fusion | flops 344064 | bytes 589826 | tf_op jit(solution)/shard_map/broadcast_in_dim | solution.py:674
  107.4 0.6 convolution_multiply_fusion
  108.0 27.6 %sum_gradients.1 = (f32[96,384]{1,0:T(8,128)S(1)}, f32[64,384]{1,0:T(8,128)S(1)}) custom-call(f32[4,2,2,96,384]{4,3,2,1,0:T(8,128)S(1)} %bitcast.94, f32[64,384]{1,0:T(8,128)S(1)} %pad.25.dk), custom_call_target="tpu_custom_call" | custom-call | tf_op jit(solution)/shard_map/sum_gradients/pallas_call | solution.py:403
  135.7 0.7 copy.32
  136.4 0.7 copy.73
  (80 shorter events, 0.4 us)
Async XLA Ops:
  2.5 0.7 copy-start.4
  40.6 1.9 %copy-start.16 = (bf16[1,2,49,384]{3,1,2,0:T(2,128)(2,1)S(1)}, bf16[1,2,49,384]{3,1,2,0:T(2,128)(2,1)}, u32[]{:S(2)}) copy-start(bf16[1,2,49,384]{3,1,2,0:T(2,128)(2,1)} %param.15) | copy-start | bytes 225796
  42.5 5.0 %copy-start.12 = (bf16[1,10,38,384]{3,2,1,0:T(8,128)(2,1)}, bf16[1,10,38,384]{3,2,1,0:T(8,128)(2,1)S(1)}, u32[]{:S(2)}) copy-start(bf16[1,10,38,384]{3,2,1,0:T(8,128)(2,1)S(1)} %pad_bitcast_fusion.3) | copy-start | bytes 875524
  43.3 4.1 %copy-start.22 = (bf16[1,1,49,384]{3,1,2,0:T(2,128)(2,1)}, bf16[1,1,49,384]{3,1,2,0:T(2,128)(2,1)S(1)}, u32[]{:S(2)}) copy-start(bf16[1,1,49,384]{3,1,2,0:T(2,128)(2,1)S(1)} %get-tuple-element.51) | copy-start | bytes 112900
  43.3 7.0 %copy-start.1 = (bf16[2,16,24,1536]{3,2,1,0:T(8,128)(2,1)S(1)}, bf16[2,16,24,1536]{3,2,1,0:T(8,128)(2,1)}, u32[]{:S(2)}) copy-start(bf16[2,16,24,1536]{3,2,1,0:T(8,128)(2,1)} %get-tuple-element.13) | copy-start | bytes 7077892
  47.5 2.9 %copy-start.2 = (f32[1,4,32,384]{3,0,2,1:T(1,128)}, f32[1,4,32,384]{3,0,2,1:T(1,128)S(1)}, u32[]{:S(2)}) copy-start(f32[1,4,32,384]{3,0,2,1:T(1,128)S(1)} %get-tuple-element.53) | copy-start | bytes 589828
  50.4 2.1 %copy-start = (bf16[2,16,96,384]{3,2,1,0:T(8,128)(2,1)S(1)}, bf16[2,16,96,384]{3,2,1,0:T(8,128)(2,1)}, u32[]{:S(2)}) copy-start(bf16[2,16,96,384]{3,2,1,0:T(8,128)(2,1)} %get-tuple-element.12) | copy-start | bytes 7077892
  52.5 1.3 copy-start.30
  52.5 1.9 %copy-start.31 = (f32[1,2,384]{2,1,0:T(2,128)S(1)}, f32[1,2,384]{2,1,0:T(2,128)}, u32[]{:S(2)}) copy-start(f32[1,2,384]{2,1,0:T(2,128)} %param.21) | copy-start | bytes 9220
  52.5 1.9 %copy-start.32 = (f32[1,2,384]{2,1,0:T(2,128)S(1)}, f32[1,2,384]{2,1,0:T(2,128)}, u32[]{:S(2)}) copy-start(f32[1,2,384]{2,1,0:T(2,128)} %param.16) | copy-start | bytes 9220
  52.5 3.1 %copy-start.3 = (f32[1,4,32,384]{3,0,2,1:T(1,128)S(1)}, f32[1,4,32,384]{3,0,2,1:T(1,128)}, u32[]{:S(2)}) copy-start(f32[1,4,32,384]{3,0,2,1:T(1,128)} %copy-done.2) | copy-start | bytes 589828
  52.5 3.5 %copy-start.24 = (f32[1,2,1536]{2,1,0:T(2,128)S(1)}, f32[1,2,1536]{2,1,0:T(2,128)}, u32[]{:S(2)}) copy-start(f32[1,2,1536]{2,1,0:T(2,128)} %param.19) | copy-start | bytes 36868
  52.5 4.1 %copy-start.17 = (bf16[4,32,384]{2,1,0:T(8,128)(2,1)S(1)}, bf16[4,32,384]{2,1,0:T(8,128)(2,1)}, u32[]{:S(2)}) copy-start(bf16[4,32,384]{2,1,0:T(8,128)(2,1)} %param.14) | copy-start | bytes 294916
  52.5 4.1 %copy-start.18 = (bf16[4,32,384]{2,1,0:T(8,128)(2,1)S(1)}, bf16[4,32,384]{2,1,0:T(8,128)(2,1)}, u32[]{:S(2)}) copy-start(bf16[4,32,384]{2,1,0:T(8,128)(2,1)} %param.13) | copy-start | bytes 294916
  55.0 0.6 copy-start.26
  56.6 1.1 copy-start.7
  56.6 1.1 copy-start.27
  56.6 1.1 copy-start.33
  57.7 2.9 %copy-start.34 = (f32[128]{0:T(128)S(1)}, f32[128]{0:T(128)}, u32[]{:S(2)}) copy-start(f32[128]{0:T(128)} %rsqrt.25) | copy-start | bytes 1540
  60.6 12.6 %copy-start.23 = (bf16[1,1,49,384]{3,1,2,0:T(2,128)(2,1)S(1)}, bf16[1,1,49,384]{3,1,2,0:T(2,128)(2,1)}, u32[]{:S(2)}) copy-start(bf16[1,1,49,384]{3,1,2,0:T(2,128)(2,1)} %copy-done.22) | copy-start | bytes 112900
  73.2 2.6 %copy-start.6 = (bf16[10,32,384]{2,1,0:T(8,128)(2,1)S(1)}, bf16[10,32,384]{2,1,0:T(8,128)(2,1)}, u32[]{:S(2)}) copy-start(bf16[10,32,384]{2,1,0:T(8,128)(2,1)} %get-tuple-element.44) | copy-start | bytes 737284
  73.2 2.7 %copy-start.20 = (bf16[1,1,49,384]{3,1,2,0:T(2,128)(2,1)S(1)}, bf16[1,1,49,384]{3,1,2,0:T(2,128)(2,1)}, u32[]{:S(2)}) copy-start(bf16[1,1,49,384]{3,1,2,0:T(2,128)(2,1)} %get-tuple-element.50) | copy-start | bytes 112900
  75.8 10.4 %collective-permute-start = (bf16[4,32,384]{2,1,0:T(8,128)(2,1)}, bf16[4,32,384]{2,1,0:T(8,128)(2,1)S(1)}, u32[]{:S(2)}, u32[]{:S(2)}) collective-permute-start(bf16[4,32,384]{2,1,0:T(8,128)(2,1)} %fusion.64), channel_id=1, source_target_pairs={{0,16},{16,0},{1,17},{17,1},{2,18},{18,2},{3,19},{19,3},{4,20},{20... | collective-permute-start | bytes 294920 | tf_op jit(solution)/shard_map/ppermute | solution.py:472
  75.9 4.2 %copy-start.14 = (bf16[1,10,38,384]{3,2,1,0:T(8,128)(2,1)}, bf16[1,10,38,384]{3,2,1,0:T(8,128)(2,1)S(1)}, u32[]{:S(2)}) copy-start(bf16[1,10,38,384]{3,2,1,0:T(8,128)(2,1)S(1)} %pad_bitcast_fusion.1) | copy-start | bytes 875524
  75.9 5.1 %copy-start.25 = (f32[384]{0:T(512)S(1)}, f32[384]{0:T(512)}, u32[]{:S(2)}) copy-start(f32[384]{0:T(512)} %get-tuple-element.64) | copy-start | bytes 4612
  75.9 5.1 %copy-start.28 = (f32[384]{0:T(512)S(1)}, f32[384]{0:T(512)}, u32[]{:S(2)}) copy-start(f32[384]{0:T(512)} %get-tuple-element.32) | copy-start | bytes 4612
  75.9 5.5 %copy-start.10 = (bf16[128,384]{1,0:T(8,128)(2,1)S(1)}, bf16[128,384]{1,0:T(8,128)(2,1)}, u32[]{:S(2)}) copy-start(bf16[128,384]{1,0:T(8,128)(2,1)} %multiply_convert_fusion.4) | copy-start | bytes 294916
  75.9 5.5 %copy-start.13 = (bf16[1,10,38,384]{3,2,1,0:T(8,128)(2,1)S(1)}, bf16[1,10,38,384]{3,2,1,0:T(8,128)(2,1)}, u32[]{:S(2)}) copy-start(bf16[1,10,38,384]{3,2,1,0:T(8,128)(2,1)} %copy-done.12) | copy-start | bytes 875524
  81.4 2.6 %copy-start.5 = (bf16[1,16,24,1536]{3,2,1,0:T(8,128)(2,1)S(1)}, bf16[1,16,24,1536]{3,2,1,0:T(8,128)(2,1)}, u32[]{:S(2)}) copy-start(bf16[1,16,24,1536]{3,2,1,0:T(8,128)(2,1)} %get-tuple-element.40) | copy-start | bytes 3538948
  81.5 2.6 %copy-start.29 = (f32[1536]{0:T(1024)S(1)}, f32[1536]{0:T(1024)}, u32[]{:S(2)}) copy-start(f32[1536]{0:T(1024)} %get-tuple-element.28) | copy-start | bytes 18436
  88.4 11.7 %copy-start.21 = (bf16[1,1,49,384]{3,1,2,0:T(2,128)(2,1)S(1)}, bf16[1,1,49,384]{3,1,2,0:T(2,128)(2,1)}, u32[]{:S(2)}) copy-start(bf16[1,1,49,384]{3,1,2,0:T(2,128)(2,1)} %get-tuple-element.50) | copy-start | bytes 112900
  100.1 2.0 %copy-start.9 = (bf16[128,1536]{1,0:T(8,128)(2,1)S(1)}, bf16[128,1536]{1,0:T(8,128)(2,1)}, u32[]{:S(2)}) copy-start(bf16[128,1536]{1,0:T(8,128)(2,1)} %get-tuple-element.43) | copy-start | bytes 1179652
  102.1 0.9 copy-start.11
  102.1 1.0 copy-start.15
  102.1 1.0 copy-start.19
  102.2 5.1 %collective-permute-start.1 = (bf16[128,1920]{1,0:T(8,128)(2,1)S(1)}, bf16[128,1920]{1,0:T(8,128)(2,1)S(1)}, u32[]{:S(2)}, u32[]{:S(2)}) collective-permute-start(bf16[128,1920]{1,0:T(8,128)(2,1)S(1)} %pad_maximum_fusion.1), channel_id=1, source_target_pairs={{0,16},{16,0},{1,17},{17,1},{2,18},{18,2},{3,19},{19,3},{4,20},{20... | collective-permute-start | bytes 1474568 | tf_op jit(solution)/shard_map/ppermute | solution.py:472
  105.3 2.1 %copy-start.8 = (bf16[128,1536]{1,0:T(8,128)(2,1)S(1)}, bf16[128,1536]{1,0:T(8,128)(2,1)}, u32[]{:S(2)}) copy-start(bf16[128,1536]{1,0:T(8,128)(2,1)} %get-tuple-element.42) | copy-start | bytes 1179652
  105.6 1.7 %collective-permute-start.2 = (bf16[49,384]{1,0:T(8,128)(2,1)S(1)}, bf16[49,384]{1,0:T(8,128)(2,1)S(1)}, u32[]{:S(2)}, u32[]{:S(2)}) collective-permute-start(bf16[49,384]{1,0:T(8,128)(2,1)S(1)} %convert_element_type.137), channel_id=1, source_target_pairs={{0,16},{16,0},{1,17},{17,1},{2,18},{18,2},{3,19},{19,3},{4,20},{20... | collective-permute-start | bytes 112904 | tf_op jit(solution)/shard_map/ppermute | solution.py:472

commit v3 on v2

--- a/solution.py
+++ b/solution.py
@@ -17,7 +17,8 @@
 def gather_kernel(
     win,
     wout,
-    x,
+    x_down,
+    x_up,
     win_all,
     wout_all,
     above,
@@ -60,12 +61,12 @@
             device_id_type=MESH,
         )
 
-    width, rows = above.shape[1], x.shape[1]
+    width, rows = above.shape[1], x_up.shape[0]
     rims = []
-    for m in (0, 1):
+    for m, x in enumerate((x_down, x_up)):
         rims.append(
             remote(
-                x.at[m, pl.ds(rows - width, width)],
+                x.at[pl.ds(rows - width, width)],
                 above.at[m],
                 rim_send.at[m, 0],
                 rim_recv.at[m, 0],
@@ -74,7 +75,7 @@
         )
         rims.append(
             remote(
-                x.at[m, pl.ds(0, width)], below.at[m], rim_send.at[m, 1], rim_recv.at[m, 1], before
+                x.at[pl.ds(0, width)], below.at[m], rim_send.at[m, 1], rim_recv.at[m, 1], before
             )
         )
 
@@ -194,12 +195,12 @@
             c.wait()
 
 
-def gathered(w_in, w_out, x, width):
+def gathered(w_in, w_out, x_down, x_up, width):
     n = lax.axis_size("space")
     p = lax.axis_index("space")
     win, wout = w_in[0], w_out[0]
     dma = pltpu.SemaphoreType.DMA
-    rim = jax.ShapeDtypeStruct((2, width) + x.shape[2:], x.dtype)
+    rim = jax.ShapeDtypeStruct((2, width) + x_up.shape[1:], x_up.dtype)
     win_all, wout_all, above, below = pl.pallas_call(
         gather_kernel,
         out_shape=(
@@ -208,7 +209,7 @@
             rim,
             rim,
         ),
-        in_specs=[pl.BlockSpec(memory_space=pl.ANY)] * 3,
+        in_specs=[pl.BlockSpec(memory_space=pl.ANY)] * 4,
         out_specs=(pl.BlockSpec(memory_space=pl.ANY),) * 4,
         scratch_shapes=[
             dma((2, 2)),
@@ -225,69 +226,17 @@
         ],
         compiler_params=pltpu.CompilerParams(collective_id=0, has_side_effects=True),
         name="gather_weights",
-    )(win, wout, x)
+    )(win, wout, x_down, x_up)
     above = jnp.where(p == 0, jnp.zeros_like(above), above)
     below = jnp.where(p == n - 1, jnp.zeros_like(below), below)
     return (
         win_all.reshape(2, n * win.shape[1], win.shape[2]),
         wout_all.reshape(2, n * wout.shape[1], wout.shape[2]),
-        jnp.concatenate([above, x, below], axis=1),
+        [
+            jnp.concatenate([above[m], x, below[m]], axis=0)
+            for m, x in enumerate((x_down, x_up))
+        ],
     )
-
-
-def rim_kernel(n, du, out, send_sem, recv_sem):
-    core = lax.axis_index("segment")
-    p = lax.axis_index("space")
-    after, before = (core, (p + 1) % n), (core, (p + n - 1) % n)
-    rows = du.shape[0]
-    width = (out.shape[0] - rows) // 2
-    barrier = pltpu.get_barrier_semaphore()
-    for device in (after, before):
-        pl.semaphore_signal(barrier, inc=1, device_id=device, device_id_type=MESH)
-    pl.semaphore_wait(barrier, 2)
-    top, bottom = pl.ds(0, width), pl.ds(width + rows, width)
-    down = pltpu.make_async_remote_copy(
-        src_ref=du.at[pl.ds(rows - width, width)],
-        dst_ref=out.at[top],
-        send_sem=send_sem.at[0],
-        recv_sem=recv_sem.at[0],
-        device_id=after,
-        device_id_type=MESH,
-    )
-    up = pltpu.make_async_remote_copy(
-        src_ref=du.at[top],
-        dst_ref=out.at[bottom],
-        send_sem=send_sem.at[1],
-        recv_sem=recv_sem.at[1],
-        device_id=before,
-        device_id_type=MESH,
-    )
-    down.start()
-    up.start()
-    out[pl.ds(width, rows)] = du[...]
-    down.wait()
-    up.wait()
-
-    @pl.when(p == 0)
-    def _():
-        out[top] = jnp.zeros((width,) + du.shape[1:], out.dtype)
-
-    @pl.when(p == n - 1)
-    def _():
-        out[bottom] = jnp.zeros((width,) + du.shape[1:], out.dtype)
-
-
-def rimmed_by_kernel(du, width):
-    n = lax.axis_size("space")
-    return pl.pallas_call(
-        functools.partial(rim_kernel, n),
-        out_shape=jax.ShapeDtypeStruct((du.shape[0] + 2 * width,) + du.shape[1:], du.dtype),
-        in_specs=[pl.BlockSpec(memory_space=pltpu.VMEM)],
-        out_specs=pl.BlockSpec(memory_space=pltpu.VMEM),
-        scratch_shapes=[pltpu.SemaphoreType.DMA((2,)), pltpu.SemaphoreType.DMA((2,))],
-        compiler_params=pltpu.CompilerParams(collective_id=2, has_side_effects=True),
-        name="gradient_rims",
-    )(du)
 
 
 def sum_kernel(
@@ -536,6 +485,35 @@
     return (du.astype(jnp.bfloat16).reshape(rows, cols, chans), hidden, outer)
 
 
+def front_kernel(v, g, gain, bias, w_first, b_first, w_second, scale_res, du, hidden, outer):
+    du[...], hidden[...], outer[...] = pointwise_back(
+        v[...], g[...], gain[...], bias[...], w_first[...], b_first[...], w_second[...], scale_res[...]
+    )
+
+
+def front_by_kernel(v, g, gain, bias, w_first, b_first, w_second, scale_res):
+    rows, cols, chans = v.shape
+    units = w_first.shape[1]
+    vmem = pl.BlockSpec(memory_space=pltpu.VMEM)
+    return pl.pallas_call(
+        front_kernel,
+        out_shape=(
+            jax.ShapeDtypeStruct(v.shape, jnp.bfloat16),
+            jax.ShapeDtypeStruct((rows * cols, units), jnp.bfloat16),
+            jax.ShapeDtypeStruct((rows * cols, chans), jnp.bfloat16),
+        ),
+        in_specs=[vmem] * 8,
+        out_specs=(vmem,) * 3,
+        compiler_params=pltpu.CompilerParams(vmem_limit_bytes=24 * 1024 * 1024),
+        cost_estimate=pl.CostEstimate(
+            flops=6 * rows * cols * chans * units,
+            bytes_accessed=4 * chans * units + 12 * rows * cols * chans,
+            transcendentals=rows * cols * units,
+        ),
+        name="pointwise_layers",
+    )(v, g, gain[None], bias[None], w_first, b_first[None], w_second, scale_res[None])
+
+
 def per_device(
     stash_down,
     stash_up,
@@ -558,7 +536,7 @@
     paired = segments == 2 and lax.axis_size("space") == 16
     if paired:
         w_in_all, w_out_all, rimmed_both = gathered(
-            w_in, w_out, jnp.concatenate([stash_down, stash_up]), half
+            w_in, w_out, stash_down[0], stash_up[0], half
         )
     else:
         w_in_all, w_out_all = (
@@ -599,7 +577,8 @@
 
         def front_live():
             v = depthwise(padded, kern)
-            return pointwise_back(
+            layers = front_by_kernel if paired else pointwise_back
+            return layers(
                 v,
                 g,
                 select(norm_gain),
@@ -618,10 +597,7 @@
             )
 
         du, hidden, outer = front_live() if paired else lax.cond(active, front_live, front_spare)
-        if paired:
-            du_rimmed = rimmed_by_kernel(du, half)
-        else:
-            du_rimmed = padded_2(du, (("space", 0),), half)
+        du_rimmed = padded_2(du, (("space", 0),), half)
 
         def back_live():
             du_pad = jnp.pad(du_rimmed.astype(jnp.float32), ((0, 0), (half, half), (0, 0)))

time: 138 us -> 106 us (0.77)
  starting transfers between devices: 0.14 us -> 12.9 us
  Pallas kernels: 83.9 us -> 71.3 us
  matrix products: 24.8 us -> 12.4 us
  local copies, waits for them, and re-layouts: 15.8 us -> 4.5 us
  other arithmetic: 11.2 us -> 2.4 us
    pallas_call x2, Pallas kernels: 19.7 us -> 2.65 us  [front_by_kernel(): pl.pallas_call(front_kernel, out_shape=(jax.ShapeDtypeStruct(v.shape, jnp...]
    ppermute x0 -> x4, starting transfers between devices: none -> 12.2 us  [the longest x2 9.57 us: padded_2(): lax.ppermute(tail, axis, [(i, (i + 1) % count) for i in range(ends)])]
    dot_general x4 -> x0, matrix products: 7.31 us -> none  [the longest x2 4.98 us: pointwise_back(): lax.dot_general(da, w_first, (((1,), (1,)), ((), ())), preferred_element_...]
    conv_general_dilated x6, matrix products: 16.9 us -> 11.8 us  [grouped_conv(): lax.conv_general_dilated(padded[None], filters, (1, 1), 'VALID', dimensio...]
    convert_element_type x7 -> x0, other arithmetic: 4.7 us -> none  [the longest x2 2.52 us: pointwise_back(): return (du.astype(jnp.bfloat16).reshape(rows, cols, chans), hidden, outer)]
    pallas_call x1, Pallas kernels: 27.6 us -> 32 us  [summed(): pl.pallas_call(sum_kernel, out_shape=(jax.ShapeDtypeStruct((share, chans)...]
    unnamed x77 -> x26, local copies, waits for them, and re-layouts: 6.07 us -> 3.6 us
    dynamic_slice x4, local copies, waits for them, and re-layouts: 2.63 us -> 0.2 us  [select(): return lax.dynamic_index_in_dim(array[0], pick, 0, keepdims=False)]
  transfers between devices with their start and end apart: 3 -> 7, of which waited for: 0 -> 2; matrix products, arithmetic and copies ran while one was open for 10% -> 9% of each run, Pallas kernels for 0% -> 0%
where the time goes in v3:
time: 106 us; the launch traced here: 105 us
  Pallas kernels  71.3 us (67%)
  starting transfers between devices  12.9 us (12%)
  matrix products  12.4 us (12%)
  local copies, waits for them, and re-layouts  4.5 us (4%)
  other arithmetic  2.4 us (2%)
  between operations  1.11 us (1%)
    pallas_call x1, Pallas kernels, gathered(): pl.pallas_call(gather_kernel, out_shape=(jax.ShapeDtypeStruct((2, n) + wi...  36.6 us
    pallas_call x1, Pallas kernels, summed(): pl.pallas_call(sum_kernel, out_shape=(jax.ShapeDtypeStruct((share, chans)...  32 us
    conv_general_dilated x6, matrix products, grouped_conv(): lax.conv_general_dilated(padded[None], filters, (1, 1), 'VALID', dimensio...  11.8 us
    ppermute x2, starting transfers between devices, padded_2(): lax.ppermute(tail, axis, [(i, (i + 1) % count) for i in range(ends)])  9.57 us
    unnamed x26, local copies, waits for them, and re-layouts  3.6 us
    pallas_call x2, Pallas kernels, front_by_kernel(): pl.pallas_call(front_kernel, out_shape=(jax.ShapeDtypeStruct(v.shape, jnp...  2.65 us
    ppermute x2, starting transfers between devices, padded_2(): lax.ppermute(head, axis, [((i + 1) % count, i) for i in range(ends)])  2.58 us
  transfers between devices with their start and end apart: 7, of which 2 were waited for; matrix products, arithmetic and copies ran while one was open for 9% of the time, Pallas kernels for 0%

profile of v3, /device:TPU:0, one launch (start us, length us, event | category | flops | bytes accessed | tf_op | source)
XLA Modules:
  0.0 105.3 jit_solution(5355934344784227998)
XLA Ops:
  0.6 0.0 copy-start.2
  0.6 0.0 copy-start.3
  0.7 0.0 copy-start.4
  0.7 36.6 %gather_weights.1 = (bf16[2,16,24,1536]{3,2,1,0:T(8,128)(2,1)}, bf16[2,16,96,384]{3,2,1,0:T(8,128)(2,1)}, bf16[2,3,32,384]{3,2,1,0:T(8,128)(2,1)}, bf16[2,3,32,384]{3,2,1,0:T(8,128)(2,1)}) custom-call(bf16[2,24,1536]{2,1,0:T(8,128)(2,1)} %bitcast.88, bf16[2,96,384]{2,1,0:T(8,128)(2,1)} %bitcast.89, bf16[4,32,384]{2,1,0:T(8,128)(2,1)} %bitcast.84, ...), custom_call_target="tpu_custom_call" | custom-call | tf_op jit(solution)/shard_map/gather_weights/pallas_call | solution.py:204
  37.3 1.0 broadcast_select_fusion.6
  38.3 0.0 copy-done.2
  38.3 0.0 copy-done.3
  38.3 0.1 broadcast_select_fusion
  38.4 0.1 pad_bitcast_fusion.1
  38.5 0.0 copy-done.4
  38.5 0.2 constant_dynamic-slice_fusion.3
  38.7 0.0 copy-start.1
  38.7 1.9 %fusion.14 = f32[1,4,32,384]{3,0,2,1:T(1,128)S(1)} fusion(bf16[7,7,1,384]{3,2,1,0:T(2,128)(2,1)S(1)} %bitcast.92, bf16[1,10,38,384]{3,2,1,0:T(8,128)(2,1)S(1)} %pad_bitcast_fusion.1), kind=kOutput, calls=%fused_computation.18 | convolution fusion | flops 4816896 | bytes 526080 | tf_op jit(solution)/shard_map/conv_general_dilated | solution.py:434
  40.6 0.0 copy-done.1
  40.6 0.0 copy-start.7
  40.6 0.0 copy-start
  40.6 0.2 fusion.37
  40.8 0.5 copy-done.7
  41.3 1.0 copy-done
  42.3 0.0 copy-start.8
  42.3 0.0 copy-start.5
  42.3 0.0 copy-start.6
  42.3 0.0 copy-start.9
  42.3 0.0 copy-start.10
  42.3 0.2 fusion.36
  42.6 0.4 copy-done.8
  43.0 0.2 copy-done.5
  43.2 0.0 copy-done.6
  43.3 0.0 copy-done.9
  43.3 0.0 copy-done.10
  43.3 1.3 %pointwise_layers.2 = (bf16[4,32,384]{2,1,0:T(8,128)(2,1)S(1)}, bf16[128,1536]{1,0:T(8,128)(2,1)S(1)}, bf16[128,384]{1,0:T(8,128)(2,1)S(1)}) custom-call(f32[4,32,384]{2,1,0:T(8,128)S(1)} %bitcast.79, bf16[4,32,384]{2,1,0:T(8,128)(2,1)S(1)} %broadcast_select_fusion.8.g, f32[1,384]{1,0:T(1,128)S(1)} %get-tuple-element.65.gain, ...), custom_call_target="tpu_custom_call" | custom-call | flops 452984832 | bytes 2949120 | tf_op jit(solution)/shard_map/pointwise_layers/pallas_call | solution.py:498
  44.7 1.3 %collective-permute-start.1 = (bf16[3,32,384]{2,1,0:T(8,128)(2,1)S(1)}, bf16[3,32,384]{2,1,0:T(8,128)(2,1)S(1)}, u32[]{:S(2)}, u32[]{:S(2)}) collective-permute-start(bf16[3,32,384]{2,1,0:T(8,128)(2,1)S(1)} %get-tuple-element.55), channel_id=1, source_target_pairs={{1,0},{2,1},{3,2},{4,3},{5,4},{6,5},{7,6},{8,7},{9,8},{10,9},{11,1... | collective-permute-start | bytes 221192 | tf_op jit(solution)/shard_map/ppermute | solution.py:397
  46.0 4.5 %collective-permute-start = (bf16[3,32,384]{2,1,0:T(8,128)(2,1)S(1)}, bf16[3,32,384]{2,1,0:T(8,128)(2,1)S(1)}, u32[]{:S(2)}, u32[]{:S(2)}) collective-permute-start(bf16[3,32,384]{2,1,0:T(8,128)(2,1)S(1)} %get-tuple-element.54), channel_id=1, source_target_pairs={{0,1},{1,2},{2,3},{3,4},{4,5},{5,6},{6,7},{7,8},{8,9},{9,10},{10,1... | collective-permute-start | bytes 221192 | tf_op jit(solution)/shard_map/ppermute | solution.py:395
  50.5 2.0 %fusion.12 = f32[1,7,7,384]{3,0,2,1:T(1,128)S(1)} fusion(bf16[1,10,38,384]{3,2,1,0:T(8,128)(2,1)S(1)} %pad_bitcast_fusion.1, bf16[4,32,1,384]{3,1,0,2:T(8,128)(2,1)S(1)} %bitcast.82), kind=kOutput, calls=%fused_computation.16 | convolution fusion | flops 4816896 | bytes 465408 | tf_op jit(solution)/shard_map/conv_general_dilated | solution.py:434
  52.5 0.1 pad_bitcast_fusion
  52.6 0.0 collective-permute-done.1
  52.6 0.3 collective-permute-done
  52.9 0.1 fusion.17
  53.0 1.9 %fusion.6 = f32[1,4,32,384]{3,0,2,1:T(1,128)S(1)} fusion(bf16[7,7,1,384]{3,2,1,0:T(2,128)(2,1)S(1)} %bitcast.93, bf16[1,10,38,384]{3,2,1,0:T(8,128)(2,1)S(1)} %fusion.17), kind=kOutput, calls=%fused_computation.9 | convolution fusion | flops 4816896 | bytes 526080 | tf_op jit(solution)/shard_map/conv_general_dilated | solution.py:434
  54.9 0.1 collective-permute-start.2
  55.0 1.9 %fusion.10 = f32[1,4,32,384]{3,0,2,1:T(1,128)S(1)} fusion(bf16[7,7,1,384]{3,2,1,0:T(2,128)(2,1)S(1)} %bitcast.90, bf16[1,10,38,384]{3,2,1,0:T(8,128)(2,1)S(1)} %pad_bitcast_fusion), kind=kOutput, calls=%fused_computation.14 | convolution fusion | flops 4816896 | bytes 526080 | tf_op jit(solution)/shard_map/conv_general_dilated | solution.py:434
  56.9 0.0 collective-permute-done.2.g
  57.0 1.3 %pointwise_layers.3 = (bf16[4,32,384]{2,1,0:T(8,128)(2,1)S(1)}, bf16[128,1536]{1,0:T(8,128)(2,1)S(1)}, bf16[128,384]{1,0:T(8,128)(2,1)S(1)}) custom-call(f32[4,32,384]{2,1,0:T(8,128)S(1)} %bitcast.80, bf16[4,32,384]{2,1,0:T(8,128)(2,1)S(1)} %collective-permute-done.2.g, f32[1,384]{1,0:T(1,128)S(1)} %get-tuple-element.64.gain, ...), custom_call_target="tpu_custom_call" | custom-call | flops 452984832 | bytes 2949120 | tf_op jit(solution)/shard_map/pointwise_layers/pallas_call | solution.py:498
  58.3 1.3 %collective-permute-start.4 = (bf16[3,32,384]{2,1,0:T(8,128)(2,1)S(1)}, bf16[3,32,384]{2,1,0:T(8,128)(2,1)S(1)}, u32[]{:S(2)}, u32[]{:S(2)}) collective-permute-start(bf16[3,32,384]{2,1,0:T(8,128)(2,1)S(1)} %get-tuple-element.53), channel_id=1, source_target_pairs={{1,0},{2,1},{3,2},{4,3},{5,4},{6,5},{7,6},{8,7},{9,8},{10,9},{11,1... | collective-permute-start | bytes 221192 | tf_op jit(solution)/shard_map/ppermute | solution.py:397
  59.6 5.0 %collective-permute-start.3 = (bf16[3,32,384]{2,1,0:T(8,128)(2,1)S(1)}, bf16[3,32,384]{2,1,0:T(8,128)(2,1)S(1)}, u32[]{:S(2)}, u32[]{:S(2)}) collective-permute-start(bf16[3,32,384]{2,1,0:T(8,128)(2,1)S(1)} %get-tuple-element.52), channel_id=1, source_target_pairs={{0,1},{1,2},{2,3},{3,4},{4,5},{5,6},{6,7},{7,8},{8,9},{9,10},{10,1... | collective-permute-start | bytes 221192 | tf_op jit(solution)/shard_map/ppermute | solution.py:395
  64.7 2.2 %fusion.26 = (f32[7,7,384]{2,1,0:T(8,128)S(1)}, bf16[1,7,7,384]{3,0,2,1:T(2,128)(2,1)S(1)}) fusion(pred[]{:T(512)S(6)} %eq.14, f32[1,7,7,384]{3,0,2,1:T(1,128)S(1)} %fusion.12, pred[]{:T(512)S(6)} %eq.17, bf16[4,32,1,384]{3,1,0,2:T(8,128)(2,1)S(1)} %bitcast.81, bf16[1,10,38,384]{3,2,1,0:T(8,128)(2,1)S(1)} %pad_bitcast_fusion), kind=kOutput, calls=%fused_computation.59 | convolution fusion | flops 4873344 | bytes 578306 | tf_op jit(solution)/shard_map/conv_general_dilated | solution.py:434
  66.9 0.2 fusion.28
  67.2 0.2 collective-permute-start.6
  67.4 0.1 select_select_fusion.1
  67.5 0.4 collective-permute-start.5
  68.0 0.5 collective-permute-done.6
  68.5 0.0 collective-permute-done.4
  68.5 0.0 collective-permute-done.3
  68.5 0.1 fusion.16
  68.6 1.9 %fusion.4 = f32[1,4,32,384]{3,0,2,1:T(1,128)S(1)} fusion(bf16[7,7,1,384]{3,2,1,0:T(2,128)(2,1)S(1)} %bitcast.91, bf16[1,10,38,384]{3,2,1,0:T(8,128)(2,1)S(1)} %fusion.16), kind=kOutput, calls=%fused_computation.7 | convolution fusion | flops 4816896 | bytes 526080 | tf_op jit(solution)/shard_map/conv_general_dilated | solution.py:434
  70.5 0.7 select_bitcast_fusion
  71.3 0.0 collective-permute-done.5
  71.3 0.6 convolution_multiply_fusion
  71.9 32.0 %sum_gradients.1 = (f32[96,384]{1,0:T(8,128)S(1)}, f32[64,384]{1,0:T(8,128)S(1)}) custom-call(f32[4,2,2,96,384]{4,3,2,1,0:T(8,128)S(1)} %bitcast.74, f32[64,384]{1,0:T(8,128)S(1)} %pad.25.dk), custom_call_target="tpu_custom_call" | custom-call | tf_op jit(solution)/shard_map/sum_gradients/pallas_call | solution.py:352
  104.0 0.7 copy.32
  104.7 0.7 copy.70
  (20 shorter events, 0.3 us)
Async XLA Ops:
  0.6 37.7 %copy-start.2 = (bf16[1,4,32,384]{3,2,1,0:T(8,128)(2,1)S(1)}, bf16[1,4,32,384]{3,2,1,0:T(8,128)(2,1)}, u32[]{:S(2)}) copy-start(bf16[1,4,32,384]{3,2,1,0:T(8,128)(2,1)} %param.11) | copy-start | bytes 294916
  0.6 37.7 %copy-start.3 = (bf16[1,4,32,384]{3,2,1,0:T(8,128)(2,1)S(1)}, bf16[1,4,32,384]{3,2,1,0:T(8,128)(2,1)}, u32[]{:S(2)}) copy-start(bf16[1,4,32,384]{3,2,1,0:T(8,128)(2,1)} %param.12) | copy-start | bytes 294916
  0.7 37.8 %copy-start.4 = (bf16[1,2,49,384]{3,1,2,0:T(2,128)(2,1)S(1)}, bf16[1,2,49,384]{3,1,2,0:T(2,128)(2,1)}, u32[]{:S(2)}) copy-start(bf16[1,2,49,384]{3,1,2,0:T(2,128)(2,1)} %param.15) | copy-start | bytes 225796
  38.7 1.9 %copy-start.1 = (bf16[2,16,24,1536]{3,2,1,0:T(8,128)(2,1)S(1)}, bf16[2,16,24,1536]{3,2,1,0:T(8,128)(2,1)}, u32[]{:S(2)}) copy-start(bf16[2,16,24,1536]{3,2,1,0:T(8,128)(2,1)} %get-tuple-element.18) | copy-start | bytes 7077892
  40.6 0.7 copy-start.7
  40.6 1.7 %copy-start = (bf16[2,16,96,384]{3,2,1,0:T(8,128)(2,1)S(1)}, bf16[2,16,96,384]{3,2,1,0:T(8,128)(2,1)}, u32[]{:S(2)}) copy-start(bf16[2,16,96,384]{3,2,1,0:T(8,128)(2,1)} %get-tuple-element.19) | copy-start | bytes 7077892
  42.3 0.7 copy-start.8
  42.3 0.9 copy-start.5
  42.3 1.0 copy-start.6
  42.3 1.0 copy-start.9
  42.3 1.0 copy-start.10
  44.7 7.9 %collective-permute-start.1 = (bf16[3,32,384]{2,1,0:T(8,128)(2,1)S(1)}, bf16[3,32,384]{2,1,0:T(8,128)(2,1)S(1)}, u32[]{:S(2)}, u32[]{:S(2)}) collective-permute-start(bf16[3,32,384]{2,1,0:T(8,128)(2,1)S(1)} %get-tuple-element.55), channel_id=1, source_target_pairs={{1,0},{2,1},{3,2},{4,3},{5,4},{6,5},{7,6},{8,7},{9,8},{10,9},{11,1... | collective-permute-start | bytes 221192 | tf_op jit(solution)/shard_map/ppermute | solution.py:397
  46.0 6.9 %collective-permute-start = (bf16[3,32,384]{2,1,0:T(8,128)(2,1)S(1)}, bf16[3,32,384]{2,1,0:T(8,128)(2,1)S(1)}, u32[]{:S(2)}, u32[]{:S(2)}) collective-permute-start(bf16[3,32,384]{2,1,0:T(8,128)(2,1)S(1)} %get-tuple-element.54), channel_id=1, source_target_pairs={{0,1},{1,2},{2,3},{3,4},{4,5},{5,6},{6,7},{7,8},{8,9},{9,10},{10,1... | collective-permute-start | bytes 221192 | tf_op jit(solution)/shard_map/ppermute | solution.py:395
  54.9 2.0 %collective-permute-start.2 = (bf16[4,32,384]{2,1,0:T(8,128)(2,1)S(1)}, bf16[4,32,384]{2,1,0:T(8,128)(2,1)S(1)}, u32[]{:S(2)}, u32[]{:S(2)}) collective-permute-start(bf16[4,32,384]{2,1,0:T(8,128)(2,1)S(1)} %fusion.23), channel_id=1, source_target_pairs={{0,16},{16,0},{1,17},{17,1},{2,18},{18,2},{3,19},{19,3},{4,20},{20... | collective-permute-start | bytes 294920 | tf_op jit(solution)/shard_map/ppermute | solution.py:421
  58.3 10.2 %collective-permute-start.4 = (bf16[3,32,384]{2,1,0:T(8,128)(2,1)S(1)}, bf16[3,32,384]{2,1,0:T(8,128)(2,1)S(1)}, u32[]{:S(2)}, u32[]{:S(2)}) collective-permute-start(bf16[3,32,384]{2,1,0:T(8,128)(2,1)S(1)} %get-tuple-element.53), channel_id=1, source_target_pairs={{1,0},{2,1},{3,2},{4,3},{5,4},{6,5},{7,6},{8,7},{9,8},{10,9},{11,1... | collective-permute-start | bytes 221192 | tf_op jit(solution)/shard_map/ppermute | solution.py:397
  59.6 8.9 %collective-permute-start.3 = (bf16[3,32,384]{2,1,0:T(8,128)(2,1)S(1)}, bf16[3,32,384]{2,1,0:T(8,128)(2,1)S(1)}, u32[]{:S(2)}, u32[]{:S(2)}) collective-permute-start(bf16[3,32,384]{2,1,0:T(8,128)(2,1)S(1)} %get-tuple-element.52), channel_id=1, source_target_pairs={{0,1},{1,2},{2,3},{3,4},{4,5},{5,6},{6,7},{7,8},{8,9},{9,10},{10,1... | collective-permute-start | bytes 221192 | tf_op jit(solution)/shard_map/ppermute | solution.py:395
  67.2 1.3 %collective-permute-start.6 = (bf16[49,384]{1,0:T(8,128)(2,1)S(1)}, bf16[49,384]{1,0:T(8,128)(2,1)S(1)}, u32[]{:S(2)}, u32[]{:S(2)}) collective-permute-start(bf16[49,384]{1,0:T(8,128)(2,1)S(1)} %convert_element_type.49), channel_id=1, source_target_pairs={{0,16},{16,0},{1,17},{17,1},{2,18},{18,2},{3,19},{19,3},{4,20},{20... | collective-permute-start | bytes 112904 | tf_op jit(solution)/shard_map/ppermute | solution.py:421
  67.5 3.7 %collective-permute-start.5 = (bf16[128,1920]{1,0:T(8,128)(2,1)S(1)}, bf16[128,1920]{1,0:T(8,128)(2,1)S(1)}, u32[]{:S(2)}, u32[]{:S(2)}) collective-permute-start(bf16[128,1920]{1,0:T(8,128)(2,1)S(1)} %pad_maximum_fusion), channel_id=1, source_target_pairs={{0,16},{16,0},{1,17},{17,1},{2,18},{18,2},{3,19},{19,3},{4,20},{20... | collective-permute-start | bytes 1474568 | tf_op jit(solution)/shard_map/ppermute | solution.py:421

commit v4 on v3

--- a/solution.py
+++ b/solution.py
@@ -286,46 +286,61 @@
         )
 
     low, high = pl.ds(0, half), pl.ds(half, half)
-    for zz in range(4):
+    order = (1, 3, 2, 0)
+    at = [(z + j) % 4 for j in range(4)]
+    first, second, third = {}, {}, []
+    waited = False
+    for j in order:
         for o in range(2):
-            sa1[zz, o] = part[zz, o, 1 - x, low].astype(sa1.dtype)
-            sb1[zz, o] = part[zz, 1 - y, o, high].astype(sb1.dtype)
-    pl.semaphore_wait(barrier, 5)
-    first = [sent(sa1, ra1, 0, over_x), sent(sb1, rb1, 1, over_y), sent(dk, kr1, 2, over_x)]
-    for c in first:
-        c.start()
-    for c in first:
-        c.wait_recv()
-    for zz in range(4):
-        sa2[zz] = (part[zz, 1 - y, x, low] + ra1[zz, 1 - y].astype(jnp.float32)).astype(sa2.dtype)
-        sb2[zz] = (part[zz, y, 1 - x, high] + rb1[zz, 1 - x].astype(jnp.float32)).astype(sb2.dtype)
+            sa1[j, o] = part[at[j], o, 1 - x, low].astype(sa1.dtype)
+            sb1[j, o] = part[at[j], 1 - y, o, high].astype(sb1.dtype)
+        if not waited:
+            pl.semaphore_wait(barrier, 5)
+            waited = True
+        first[j] = (
+            sent(sa1.at[j], ra1.at[j], j, over_x),
+            sent(sb1.at[j], rb1.at[j], 4 + j, over_y),
+        )
+        for c in first[j]:
+            c.start()
+    dk_first = sent(dk, kr1, 22, over_x)
+    dk_first.start()
+    for j in order:
+        for c in first[j]:
+            c.wait_recv()
+        sa2[j] = (part[at[j], 1 - y, x, low] + ra1[j, 1 - y].astype(jnp.float32)).astype(sa2.dtype)
+        sb2[j] = (part[at[j], y, 1 - x, high] + rb1[j, 1 - x].astype(jnp.float32)).astype(sb2.dtype)
+        second[j] = (
+            sent(sa2.at[j], ra2.at[j], 8 + j, over_y),
+            sent(sb2.at[j], rb2.at[j], 12 + j, over_x),
+        )
+        for c in second[j]:
+            c.start()
+    dk_first.wait_recv()
     ks2[...] = dk[...] + kr1[...]
-    second = [sent(sa2, ra2, 3, over_y), sent(sb2, rb2, 4, over_x), sent(ks2, kr2, 5, over_y)]
-    for c in second:
-        c.start()
-
-    def kept(zz):
-        a = part[zz, y, x, low] + ra1[zz, y].astype(jnp.float32)
-        b = part[zz, y, x, high] + rb1[zz, x].astype(jnp.float32)
-        return a, b
-
-    for c in second:
-        c.wait_recv()
+    dk_second = sent(ks2, kr2, 23, over_y)
+    dk_second.start()
+
+    def kept(j):
+        for c in second[j]:
+            c.wait_recv()
+        a = part[at[j], y, x, low] + ra1[j, y].astype(jnp.float32)
+        b = part[at[j], y, x, high] + rb1[j, x].astype(jnp.float32)
+        return a + ra2[j].astype(jnp.float32), b + rb2[j].astype(jnp.float32)
+
+    for j in (1, 3, 2):
+        a, b = kept(j)
+        s3[j - 1, low] = a.astype(s3.dtype)
+        s3[j - 1, high] = b.astype(s3.dtype)
+        third.append(sent(s3.at[j - 1], r3.at[j - 1], 15 + j, over_z[j - 1]))
+        third[-1].start()
+    a, b = kept(0)
+    dk_second.wait_recv()
     ksum = ks2[...] + kr2[...]
     ks3[...] = ksum.astype(ks3.dtype)
-    third = []
-    for j in (1, 2, 3):
-        zz = (z + j) % 4
-        a, b = kept(zz)
-        s3[j - 1, low] = (a + ra2[zz].astype(jnp.float32)).astype(s3.dtype)
-        s3[j - 1, high] = (b + rb2[zz].astype(jnp.float32)).astype(s3.dtype)
-        third.append(sent(s3.at[j - 1], r3.at[j - 1], 6 + j, over_z[j - 1]))
-        third.append(sent(ks3, kr3.at[j - 1], 9 + j, over_z[j - 1]))
-        third[-2].start()
+    for j in (1, 3, 2):
+        third.append(sent(ks3, kr3.at[j - 1], 18 + j, over_z[j - 1]))
         third[-1].start()
-    a, b = kept(z)
-    a = a + ra2[z].astype(jnp.float32)
-    b = b + rb2[z].astype(jnp.float32)
     for c in third:
         c.wait_recv()
     for j in range(3):
@@ -335,7 +350,10 @@
     out[low] = a
     out[high] = b
     dk_out[...] = ksum
-    for c in first + second + third:
+    for j in order:
+        for c in first[j] + second[j]:
+            c.wait_send()
+    for c in [dk_first, dk_second] + third:
         c.wait_send()
 
 
@@ -373,8 +391,8 @@
             pltpu.VMEM(dk.shape, jnp.float32),
             pltpu.VMEM(dk.shape, sent),
             pltpu.VMEM((3,) + dk.shape, sent),
-            pltpu.SemaphoreType.DMA((13,)),
-            pltpu.SemaphoreType.DMA((13,)),
+            pltpu.SemaphoreType.DMA((24,)),
+            pltpu.SemaphoreType.DMA((24,)),
         ],
         compiler_params=pltpu.CompilerParams(
             collective_id=1, has_side_effects=True, vmem_limit_bytes=24 * 1024 * 1024

time: 106 us -> 102 us (0.962)
  Pallas kernels: 71.3 us -> 67.4 us
    pallas_call x1, Pallas kernels: 32 us -> 28.2 us  [summed(): pl.pallas_call(sum_kernel, out_shape=(jax.ShapeDtypeStruct((share, chans)...]
where the time goes in v4:
time: 102 us; the launch traced here: 101 us
  Pallas kernels  67.4 us (66%)
  starting transfers between devices  12.9 us (13%)
  matrix products  12.4 us (12%)
  local copies, waits for them, and re-layouts  4.5 us (4%)
  other arithmetic  2.4 us (2%)
  between operations  1.11 us (1%)
    pallas_call x1, Pallas kernels, gathered(): pl.pallas_call(gather_kernel, out_shape=(jax.ShapeDtypeStruct((2, n) + wi...  36.6 us
    pallas_call x1, Pallas kernels, summed(): pl.pallas_call(sum_kernel, out_shape=(jax.ShapeDtypeStruct((share, chans)...  28.2 us
    conv_general_dilated x6, matrix products, grouped_conv(): lax.conv_general_dilated(padded[None], filters, (1, 1), 'VALID', dimensio...  11.8 us
    ppermute x2, starting transfers between devices, padded_2(): lax.ppermute(tail, axis, [(i, (i + 1) % count) for i in range(ends)])  9.57 us
    unnamed x26, local copies, waits for them, and re-layouts  3.6 us
    pallas_call x2, Pallas kernels, front_by_kernel(): pl.pallas_call(front_kernel, out_shape=(jax.ShapeDtypeStruct(v.shape, jnp...  2.65 us
    ppermute x2, starting transfers between devices, padded_2(): lax.ppermute(head, axis, [((i + 1) % count, i) for i in range(ends)])  2.58 us
  transfers between devices with their start and end apart: 7, of which 2 were waited for; matrix products, arithmetic and copies ran while one was open for 9% of the time, Pallas kernels for 0%

profile of v4, /device:TPU:0, one launch (start us, length us, event | category | flops | bytes accessed | tf_op | source)
XLA Modules:
  0.0 101.5 jit_solution(16168450198385193354)
XLA Ops:
  0.6 0.0 copy-start.2
  0.6 0.0 copy-start.3
  0.7 0.0 copy-start.4
  0.7 36.6 %gather_weights.1 = (bf16[2,16,24,1536]{3,2,1,0:T(8,128)(2,1)}, bf16[2,16,96,384]{3,2,1,0:T(8,128)(2,1)}, bf16[2,3,32,384]{3,2,1,0:T(8,128)(2,1)}, bf16[2,3,32,384]{3,2,1,0:T(8,128)(2,1)}) custom-call(bf16[2,24,1536]{2,1,0:T(8,128)(2,1)} %bitcast.88, bf16[2,96,384]{2,1,0:T(8,128)(2,1)} %bitcast.89, bf16[4,32,384]{2,1,0:T(8,128)(2,1)} %bitcast.84, ...), custom_call_target="tpu_custom_call" | custom-call | tf_op jit(solution)/shard_map/gather_weights/pallas_call | solution.py:204
  37.3 1.0 broadcast_select_fusion.6
  38.3 0.0 copy-done.2
  38.3 0.0 copy-done.3
  38.3 0.1 broadcast_select_fusion
  38.4 0.1 pad_bitcast_fusion.1
  38.5 0.0 copy-done.4
  38.5 0.2 constant_dynamic-slice_fusion.3
  38.7 0.0 copy-start.1
  38.7 1.9 %fusion.14 = f32[1,4,32,384]{3,0,2,1:T(1,128)S(1)} fusion(bf16[7,7,1,384]{3,2,1,0:T(2,128)(2,1)S(1)} %bitcast.92, bf16[1,10,38,384]{3,2,1,0:T(8,128)(2,1)S(1)} %pad_bitcast_fusion.1), kind=kOutput, calls=%fused_computation.18 | convolution fusion | flops 4816896 | bytes 526080 | tf_op jit(solution)/shard_map/conv_general_dilated | solution.py:452
  40.6 0.0 copy-done.1
  40.6 0.0 copy-start.7
  40.6 0.0 copy-start
  40.6 0.2 fusion.37
  40.8 0.5 copy-done.7
  41.3 1.0 copy-done
  42.3 0.0 copy-start.8
  42.3 0.0 copy-start.5
  42.3 0.0 copy-start.6
  42.3 0.0 copy-start.9
  42.3 0.0 copy-start.10
  42.3 0.2 fusion.36
  42.6 0.4 copy-done.8
  43.0 0.2 copy-done.5
  43.2 0.0 copy-done.6
  43.3 0.0 copy-done.9
  43.3 0.0 copy-done.10
  43.3 1.3 %pointwise_layers.2 = (bf16[4,32,384]{2,1,0:T(8,128)(2,1)S(1)}, bf16[128,1536]{1,0:T(8,128)(2,1)S(1)}, bf16[128,384]{1,0:T(8,128)(2,1)S(1)}) custom-call(f32[4,32,384]{2,1,0:T(8,128)S(1)} %bitcast.79, bf16[4,32,384]{2,1,0:T(8,128)(2,1)S(1)} %broadcast_select_fusion.8.g, f32[1,384]{1,0:T(1,128)S(1)} %get-tuple-element.65.gain, ...), custom_call_target="tpu_custom_call" | custom-call | flops 452984832 | bytes 2949120 | tf_op jit(solution)/shard_map/pointwise_layers/pallas_call | solution.py:516
  44.7 1.3 %collective-permute-start.1 = (bf16[3,32,384]{2,1,0:T(8,128)(2,1)S(1)}, bf16[3,32,384]{2,1,0:T(8,128)(2,1)S(1)}, u32[]{:S(2)}, u32[]{:S(2)}) collective-permute-start(bf16[3,32,384]{2,1,0:T(8,128)(2,1)S(1)} %get-tuple-element.55), channel_id=1, source_target_pairs={{1,0},{2,1},{3,2},{4,3},{5,4},{6,5},{7,6},{8,7},{9,8},{10,9},{11,1... | collective-permute-start | bytes 221192 | tf_op jit(solution)/shard_map/ppermute | solution.py:415
  46.0 4.5 %collective-permute-start = (bf16[3,32,384]{2,1,0:T(8,128)(2,1)S(1)}, bf16[3,32,384]{2,1,0:T(8,128)(2,1)S(1)}, u32[]{:S(2)}, u32[]{:S(2)}) collective-permute-start(bf16[3,32,384]{2,1,0:T(8,128)(2,1)S(1)} %get-tuple-element.54), channel_id=1, source_target_pairs={{0,1},{1,2},{2,3},{3,4},{4,5},{5,6},{6,7},{7,8},{8,9},{9,10},{10,1... | collective-permute-start | bytes 221192 | tf_op jit(solution)/shard_map/ppermute | solution.py:413
  50.5 2.0 %fusion.12 = f32[1,7,7,384]{3,0,2,1:T(1,128)S(1)} fusion(bf16[1,10,38,384]{3,2,1,0:T(8,128)(2,1)S(1)} %pad_bitcast_fusion.1, bf16[4,32,1,384]{3,1,0,2:T(8,128)(2,1)S(1)} %bitcast.82), kind=kOutput, calls=%fused_computation.16 | convolution fusion | flops 4816896 | bytes 465408 | tf_op jit(solution)/shard_map/conv_general_dilated | solution.py:452
  52.5 0.1 pad_bitcast_fusion
  52.6 0.0 collective-permute-done.1
  52.6 0.3 collective-permute-done
  52.9 0.1 fusion.17
  53.0 1.9 %fusion.6 = f32[1,4,32,384]{3,0,2,1:T(1,128)S(1)} fusion(bf16[7,7,1,384]{3,2,1,0:T(2,128)(2,1)S(1)} %bitcast.93, bf16[1,10,38,384]{3,2,1,0:T(8,128)(2,1)S(1)} %fusion.17), kind=kOutput, calls=%fused_computation.9 | convolution fusion | flops 4816896 | bytes 526080 | tf_op jit(solution)/shard_map/conv_general_dilated | solution.py:452
  54.9 0.1 collective-permute-start.2
  55.0 1.9 %fusion.10 = f32[1,4,32,384]{3,0,2,1:T(1,128)S(1)} fusion(bf16[7,7,1,384]{3,2,1,0:T(2,128)(2,1)S(1)} %bitcast.90, bf16[1,10,38,384]{3,2,1,0:T(8,128)(2,1)S(1)} %pad_bitcast_fusion), kind=kOutput, calls=%fused_computation.14 | convolution fusion | flops 4816896 | bytes 526080 | tf_op jit(solution)/shard_map/conv_general_dilated | solution.py:452
  56.9 0.0 collective-permute-done.2.g
  57.0 1.3 %pointwise_layers.3 = (bf16[4,32,384]{2,1,0:T(8,128)(2,1)S(1)}, bf16[128,1536]{1,0:T(8,128)(2,1)S(1)}, bf16[128,384]{1,0:T(8,128)(2,1)S(1)}) custom-call(f32[4,32,384]{2,1,0:T(8,128)S(1)} %bitcast.80, bf16[4,32,384]{2,1,0:T(8,128)(2,1)S(1)} %collective-permute-done.2.g, f32[1,384]{1,0:T(1,128)S(1)} %get-tuple-element.64.gain, ...), custom_call_target="tpu_custom_call" | custom-call | flops 452984832 | bytes 2949120 | tf_op jit(solution)/shard_map/pointwise_layers/pallas_call | solution.py:516
  58.3 1.3 %collective-permute-start.4 = (bf16[3,32,384]{2,1,0:T(8,128)(2,1)S(1)}, bf16[3,32,384]{2,1,0:T(8,128)(2,1)S(1)}, u32[]{:S(2)}, u32[]{:S(2)}) collective-permute-start(bf16[3,32,384]{2,1,0:T(8,128)(2,1)S(1)} %get-tuple-element.53), channel_id=1, source_target_pairs={{1,0},{2,1},{3,2},{4,3},{5,4},{6,5},{7,6},{8,7},{9,8},{10,9},{11,1... | collective-permute-start | bytes 221192 | tf_op jit(solution)/shard_map/ppermute | solution.py:415
  59.6 5.0 %collective-permute-start.3 = (bf16[3,32,384]{2,1,0:T(8,128)(2,1)S(1)}, bf16[3,32,384]{2,1,0:T(8,128)(2,1)S(1)}, u32[]{:S(2)}, u32[]{:S(2)}) collective-permute-start(bf16[3,32,384]{2,1,0:T(8,128)(2,1)S(1)} %get-tuple-element.52), channel_id=1, source_target_pairs={{0,1},{1,2},{2,3},{3,4},{4,5},{5,6},{6,7},{7,8},{8,9},{9,10},{10,1... | collective-permute-start | bytes 221192 | tf_op jit(solution)/shard_map/ppermute | solution.py:413
  64.7 2.2 %fusion.26 = (f32[7,7,384]{2,1,0:T(8,128)S(1)}, bf16[1,7,7,384]{3,0,2,1:T(2,128)(2,1)S(1)}) fusion(pred[]{:T(512)S(6)} %eq.14, f32[1,7,7,384]{3,0,2,1:T(1,128)S(1)} %fusion.12, pred[]{:T(512)S(6)} %eq.17, bf16[4,32,1,384]{3,1,0,2:T(8,128)(2,1)S(1)} %bitcast.81, bf16[1,10,38,384]{3,2,1,0:T(8,128)(2,1)S(1)} %pad_bitcast_fusion), kind=kOutput, calls=%fused_computation.59 | convolution fusion | flops 4873344 | bytes 578306 | tf_op jit(solution)/shard_map/conv_general_dilated | solution.py:452
  66.9 0.2 fusion.28
  67.2 0.2 collective-permute-start.6
  67.4 0.1 select_select_fusion.1
  67.5 0.4 collective-permute-start.5
  68.0 0.5 collective-permute-done.6
  68.5 0.0 collective-permute-done.4
  68.5 0.0 collective-permute-done.3
  68.5 0.1 fusion.16
  68.6 1.9 %fusion.4 = f32[1,4,32,384]{3,0,2,1:T(1,128)S(1)} fusion(bf16[7,7,1,384]{3,2,1,0:T(2,128)(2,1)S(1)} %bitcast.91, bf16[1,10,38,384]{3,2,1,0:T(8,128)(2,1)S(1)} %fusion.16), kind=kOutput, calls=%fused_computation.7 | convolution fusion | flops 4816896 | bytes 526080 | tf_op jit(solution)/shard_map/conv_general_dilated | solution.py:452
  70.5 0.7 select_bitcast_fusion
  71.3 0.0 collective-permute-done.5
  71.3 0.6 convolution_multiply_fusion
  71.9 28.2 %sum_gradients.1 = (f32[96,384]{1,0:T(8,128)S(1)}, f32[64,384]{1,0:T(8,128)S(1)}) custom-call(f32[4,2,2,96,384]{4,3,2,1,0:T(8,128)S(1)} %bitcast.74, f32[64,384]{1,0:T(8,128)S(1)} %pad.25.dk), custom_call_target="tpu_custom_call" | custom-call | tf_op jit(solution)/shard_map/sum_gradients/pallas_call | solution.py:370
  100.1 0.7 copy.32
  100.8 0.7 copy.70
  (20 shorter events, 0.3 us)
Async XLA Ops:
  0.6 37.7 %copy-start.2 = (bf16[1,4,32,384]{3,2,1,0:T(8,128)(2,1)S(1)}, bf16[1,4,32,384]{3,2,1,0:T(8,128)(2,1)}, u32[]{:S(2)}) copy-start(bf16[1,4,32,384]{3,2,1,0:T(8,128)(2,1)} %param.11) | copy-start | bytes 294916
  0.6 37.7 %copy-start.3 = (bf16[1,4,32,384]{3,2,1,0:T(8,128)(2,1)S(1)}, bf16[1,4,32,384]{3,2,1,0:T(8,128)(2,1)}, u32[]{:S(2)}) copy-start(bf16[1,4,32,384]{3,2,1,0:T(8,128)(2,1)} %param.12) | copy-start | bytes 294916
  0.7 37.8 %copy-start.4 = (bf16[1,2,49,384]{3,1,2,0:T(2,128)(2,1)S(1)}, bf16[1,2,49,384]{3,1,2,0:T(2,128)(2,1)}, u32[]{:S(2)}) copy-start(bf16[1,2,49,384]{3,1,2,0:T(2,128)(2,1)} %param.15) | copy-start | bytes 225796
  38.7 1.9 %copy-start.1 = (bf16[2,16,24,1536]{3,2,1,0:T(8,128)(2,1)S(1)}, bf16[2,16,24,1536]{3,2,1,0:T(8,128)(2,1)}, u32[]{:S(2)}) copy-start(bf16[2,16,24,1536]{3,2,1,0:T(8,128)(2,1)} %get-tuple-element.18) | copy-start | bytes 7077892
  40.6 0.7 copy-start.7
  40.6 1.7 %copy-start = (bf16[2,16,96,384]{3,2,1,0:T(8,128)(2,1)S(1)}, bf16[2,16,96,384]{3,2,1,0:T(8,128)(2,1)}, u32[]{:S(2)}) copy-start(bf16[2,16,96,384]{3,2,1,0:T(8,128)(2,1)} %get-tuple-element.19) | copy-start | bytes 7077892
  42.3 0.7 copy-start.8
  42.3 0.9 copy-start.5
  42.3 1.0 copy-start.6
  42.3 1.0 copy-start.9
  42.3 1.0 copy-start.10
  44.7 7.9 %collective-permute-start.1 = (bf16[3,32,384]{2,1,0:T(8,128)(2,1)S(1)}, bf16[3,32,384]{2,1,0:T(8,128)(2,1)S(1)}, u32[]{:S(2)}, u32[]{:S(2)}) collective-permute-start(bf16[3,32,384]{2,1,0:T(8,128)(2,1)S(1)} %get-tuple-element.55), channel_id=1, source_target_pairs={{1,0},{2,1},{3,2},{4,3},{5,4},{6,5},{7,6},{8,7},{9,8},{10,9},{11,1... | collective-permute-start | bytes 221192 | tf_op jit(solution)/shard_map/ppermute | solution.py:415
  46.0 6.9 %collective-permute-start = (bf16[3,32,384]{2,1,0:T(8,128)(2,1)S(1)}, bf16[3,32,384]{2,1,0:T(8,128)(2,1)S(1)}, u32[]{:S(2)}, u32[]{:S(2)}) collective-permute-start(bf16[3,32,384]{2,1,0:T(8,128)(2,1)S(1)} %get-tuple-element.54), channel_id=1, source_target_pairs={{0,1},{1,2},{2,3},{3,4},{4,5},{5,6},{6,7},{7,8},{8,9},{9,10},{10,1... | collective-permute-start | bytes 221192 | tf_op jit(solution)/shard_map/ppermute | solution.py:413
  54.9 2.0 %collective-permute-start.2 = (bf16[4,32,384]{2,1,0:T(8,128)(2,1)S(1)}, bf16[4,32,384]{2,1,0:T(8,128)(2,1)S(1)}, u32[]{:S(2)}, u32[]{:S(2)}) collective-permute-start(bf16[4,32,384]{2,1,0:T(8,128)(2,1)S(1)} %fusion.23), channel_id=1, source_target_pairs={{0,16},{16,0},{1,17},{17,1},{2,18},{18,2},{3,19},{19,3},{4,20},{20... | collective-permute-start | bytes 294920 | tf_op jit(solution)/shard_map/ppermute | solution.py:439
  58.3 10.2 %collective-permute-start.4 = (bf16[3,32,384]{2,1,0:T(8,128)(2,1)S(1)}, bf16[3,32,384]{2,1,0:T(8,128)(2,1)S(1)}, u32[]{:S(2)}, u32[]{:S(2)}) collective-permute-start(bf16[3,32,384]{2,1,0:T(8,128)(2,1)S(1)} %get-tuple-element.53), channel_id=1, source_target_pairs={{1,0},{2,1},{3,2},{4,3},{5,4},{6,5},{7,6},{8,7},{9,8},{10,9},{11,1... | collective-permute-start | bytes 221192 | tf_op jit(solution)/shard_map/ppermute | solution.py:415
  59.6 8.9 %collective-permute-start.3 = (bf16[3,32,384]{2,1,0:T(8,128)(2,1)S(1)}, bf16[3,32,384]{2,1,0:T(8,128)(2,1)S(1)}, u32[]{:S(2)}, u32[]{:S(2)}) collective-permute-start(bf16[3,32,384]{2,1,0:T(8,128)(2,1)S(1)} %get-tuple-element.52), channel_id=1, source_target_pairs={{0,1},{1,2},{2,3},{3,4},{4,5},{5,6},{6,7},{7,8},{8,9},{9,10},{10,1... | collective-permute-start | bytes 221192 | tf_op jit(solution)/shard_map/ppermute | solution.py:413
  67.2 1.3 %collective-permute-start.6 = (bf16[49,384]{1,0:T(8,128)(2,1)S(1)}, bf16[49,384]{1,0:T(8,128)(2,1)S(1)}, u32[]{:S(2)}, u32[]{:S(2)}) collective-permute-start(bf16[49,384]{1,0:T(8,128)(2,1)S(1)} %convert_element_type.49), channel_id=1, source_target_pairs={{0,16},{16,0},{1,17},{17,1},{2,18},{18,2},{3,19},{19,3},{4,20},{20... | collective-permute-start | bytes 112904 | tf_op jit(solution)/shard_map/ppermute | solution.py:439
  67.5 3.7 %collective-permute-start.5 = (bf16[128,1920]{1,0:T(8,128)(2,1)S(1)}, bf16[128,1920]{1,0:T(8,128)(2,1)S(1)}, u32[]{:S(2)}, u32[]{:S(2)}) collective-permute-start(bf16[128,1920]{1,0:T(8,128)(2,1)S(1)} %pad_maximum_fusion), channel_id=1, source_target_pairs={{0,16},{16,0},{1,17},{17,1},{2,18},{18,2},{3,19},{19,3},{4,20},{20... | collective-permute-start | bytes 1474568 | tf_op jit(solution)/shard_map/ppermute | solution.py:439
